TPU v7x, 32 devices: a whole 2x2x4 slice. The times are simulated.
32 devices in a mesh: az: 8 (over z, core), rg: 4 (over y, x).
Axes of the slice: x: 2, y: 2, z: 4, core: 2. Of those that a mesh axis runs over, the one named last changes fastest.
Arguments:
- raw_echoes: float32 [128, 4, 2, 8192], P(('az', 'rg')), may hold values from -6 to 6
- chirp_spectrum: float32 [2, 8192], replicated, may hold values from -5 to 5
- reconstruction: float32 [2, 4, 4, 128], replicated, may hold values from -2 to 2
- delays: int32 [4], replicated, may hold values from 0 to 127
- azimuth_rate: float32 [8192], P(('az', 'rg')), may hold values from 0.5 to 2
- band_halfwidth: int32 [8192], P(('az', 'rg')), may hold values from 64 to 256
- migration: int32 [8192], P(('az', 'rg')), may hold values from 8 to 16
Outputs:
- focused_image: float32 [2, 8192, 512], P(None, ('az', 'rg'))
All inputs are finite; a program needn't handle non-finite values.
Results may differ from a plain program's by a relative error of at most 0.00007.
Values sent between devices are 32-bit elements; how exact they have to be, the bound alone decides.
A program may use at most 64 MiB of HBM per device.

v0:
```python
import math

import jax
import jax.numpy as jnp
from jax import lax
from jax.sharding import PartitionSpec as P

MIG = 16


highest = lax.Precision.HIGHEST
curvature = 32.0


def passed_along(value, axis, by):
    size = lax.axis_size(axis)
    pairs = [(i, i + by) for i in range(size) if 0 <= i + by < size]
    return lax.ppermute(value, axis, pairs)


def factor_pair(length):
    largest = 1
    for candidate in range(1, length + 1):
        if candidate * candidate > length:
            break
        if length % candidate == 0:
            largest = candidate
    return (largest, length // largest)


def dft_matrix(length, direction):
    indices = jnp.arange(length, dtype=jnp.int32)
    angles = (
        2.0 * math.pi / length * (indices[:, None] * indices[None, :] % length).astype(jnp.float32)
    )
    cosine = jnp.cos(angles)
    sines = direction * jnp.sin(angles)
    return jnp.stack(
        [jnp.stack([cosine, -sines], axis=1), jnp.stack([sines, cosine], axis=1)], axis=0
    )


def twiddle(lead_size, trail_size, length, direction):
    lead_index = jnp.arange(lead_size, dtype=jnp.int32)
    trail_index = jnp.arange(trail_size, dtype=jnp.int32)
    angles = (
        2.0
        * math.pi
        / length
        * (lead_index[:, None] * trail_index[None, :] % length).astype(jnp.float32)
    )
    return (jnp.cos(angles), direction * jnp.sin(angles))


def complex_mul(values, factor_real, factor_imag, part_axis):
    real_part = lax.index_in_dim(values, 0, part_axis, keepdims=True)
    imag_part = lax.index_in_dim(values, 1, part_axis, keepdims=True)
    return jnp.concatenate(
        [
            real_part * factor_real - imag_part * factor_imag,
            real_part * factor_imag + imag_part * factor_real,
        ],
        axis=part_axis,
    )


def range_focus(raw_echoes, chirp_spectrum):
    local_pulses, channels, _, length = raw_echoes.shape
    lead_size, trail_size = factor_pair(length)
    layout = raw_echoes.reshape(local_pulses, channels, 2, lead_size, trail_size)
    sectioned = jnp.einsum(
        "okci,pqcij->pqokj", dft_matrix(lead_size, -1.0), layout, precision=highest
    )
    twiddle_real, twiddle_imag = twiddle(lead_size, trail_size, length, -1.0)
    sectioned = complex_mul(sectioned, twiddle_real, twiddle_imag, 2)
    spectrum = jnp.einsum(
        "olcj,pqckj->pqolk", dft_matrix(trail_size, -1.0), sectioned, precision=highest
    )
    spectrum = spectrum.reshape(local_pulses, channels, 2, length)
    spectrum = complex_mul(spectrum, chirp_spectrum[0], -chirp_spectrum[1], 2)
    layout = spectrum.reshape(local_pulses, channels, 2, lead_size, trail_size)
    sectioned = jnp.einsum(
        "okci,pqcij->pqokj", dft_matrix(lead_size, 1.0), layout, precision=highest
    )
    twiddle_real, twiddle_imag = twiddle(lead_size, trail_size, length, 1.0)
    sectioned = complex_mul(sectioned, twiddle_real, twiddle_imag, 2)
    restored = jnp.einsum(
        "olcj,pqckj->qoplk", dft_matrix(trail_size, 1.0), sectioned, precision=highest
    )
    return restored.reshape(channels, 2, local_pulses, length) / length


def reconstruct(turned, mixing_real, mixing_imag):
    channels, _, local_pulses, blocks, bin_count = turned.shape
    pulse_total = blocks * local_pulses
    sectioned = jnp.einsum("okcm,qcimb->qobik", dft_matrix(blocks, -1.0), turned, precision=highest)
    twiddle_real, twiddle_imag = twiddle(local_pulses, blocks, pulse_total, -1.0)
    sectioned = complex_mul(sectioned, twiddle_real, twiddle_imag, 1)
    spectrum = jnp.einsum(
        "olci,qcbik->qoblk", dft_matrix(local_pulses, -1.0), sectioned, precision=highest
    )
    spectrum = spectrum.reshape(channels, 2, bin_count, pulse_total) / math.sqrt(pulse_total)
    spec_real = spectrum[:, 0]
    spec_imag = spectrum[:, 1]
    unfolded_real = jnp.einsum(
        "bcf,crf->rbf", mixing_real, spec_real, precision=highest
    ) - jnp.einsum("bcf,crf->rbf", mixing_imag, spec_imag, precision=highest)
    unfolded_imag = jnp.einsum(
        "bcf,crf->rbf", mixing_real, spec_imag, precision=highest
    ) + jnp.einsum("bcf,crf->rbf", mixing_imag, spec_real, precision=highest)
    unfolded = jnp.stack([unfolded_real, unfolded_imag], axis=0)
    return unfolded.reshape(2, bin_count, channels * pulse_total)


def azimuth_focus(unfolded, azimuth_rate, band_halfwidth, migration):
    bin_count = azimuth_rate.shape[0]
    length = unfolded.shape[2]
    doppler_index = jnp.arange(length, dtype=jnp.int32)
    centred = doppler_index - length * (doppler_index >= length // 2).astype(jnp.int32)
    band_square = band_halfwidth * band_halfwidth
    squared = jnp.minimum((centred * centred)[None, :], band_square[:, None])
    migration_shift = (migration[:, None] * squared + (band_square // 2)[:, None]) // band_square[
        :, None
    ]
    migrated = jnp.zeros((2, bin_count, length), jnp.float32)
    for offset in range(MIG + 1):
        window = unfolded[:, offset : offset + bin_count, :]
        migrated = jnp.where((migration_shift == offset)[None], window, migrated)
    relative = centred.astype(jnp.float32) / (length // 2)
    matched_phase = math.pi * curvature * azimuth_rate[:, None] * (relative * relative)[None, :]
    focused = complex_mul(migrated, jnp.cos(matched_phase), jnp.sin(matched_phase), 0)
    inside = jnp.abs(centred)[None, :] < band_halfwidth[:, None]
    focused = jnp.where(inside[None], focused, 0.0)
    lead_size, trail_size = factor_pair(length)
    layout = focused.reshape(2, bin_count, lead_size, trail_size)
    sectioned = jnp.einsum("okci,cbij->obkj", dft_matrix(lead_size, 1.0), layout, precision=highest)
    twiddle_real, twiddle_imag = twiddle(lead_size, trail_size, length, 1.0)
    sectioned = complex_mul(sectioned, twiddle_real, twiddle_imag, 0)
    focused_image = jnp.einsum(
        "olcj,cbkj->oblk", dft_matrix(trail_size, 1.0), sectioned, precision=highest
    )
    return focused_image.reshape(2, bin_count, length) / math.sqrt(length)


def local(
    raw_echoes, chirp_spectrum, reconstruction, delays, azimuth_rate, band_halfwidth, migration
):
    compressed = range_focus(raw_echoes, chirp_spectrum)
    channels, _, local_pulses, length = compressed.shape
    azimuth_count = lax.axis_size("az")
    range_count = lax.axis_size("rg")
    bin_count = length // (azimuth_count * range_count)
    layout = compressed.reshape(channels, 2, local_pulses, azimuth_count, range_count, bin_count)
    layout = lax.all_to_all(layout, "rg", split_axis=4, concat_axis=4, tiled=True)
    layout = lax.all_to_all(layout, "az", split_axis=3, concat_axis=3, tiled=True)
    turned = layout.reshape(channels, 2, local_pulses, azimuth_count * range_count, bin_count)
    pulse_total = azimuth_count * range_count * local_pulses
    frequency = jnp.arange(pulse_total, dtype=jnp.int32)
    angles = (
        2.0
        * math.pi
        / pulse_total
        * (frequency[None, :] * delays[:, None] % pulse_total).astype(jnp.float32)
    )
    align_real = jnp.cos(angles)[None]
    align_imag = jnp.sin(angles)[None]
    mixing_real = reconstruction[0] * align_real - reconstruction[1] * align_imag
    mixing_imag = reconstruction[0] * align_imag + reconstruction[1] * align_real
    unfolded = reconstruct(turned, mixing_real, mixing_imag)
    margin_bins = passed_along(unfolded[:, :MIG, :], ("az", "rg"), -1)
    unfolded = jnp.concatenate([unfolded, margin_bins], axis=1)
    return azimuth_focus(unfolded, azimuth_rate, band_halfwidth, migration)


def solution(mesh):
    in_specs = (
        P(("az", "rg"), None, None, None),
        P(),
        P(),
        P(),
        P(("az", "rg")),
        P(("az", "rg")),
        P(("az", "rg")),
    )
    out_specs = P(None, ("az", "rg"), None)
    return jax.shard_map(local, mesh=mesh, in_specs=in_specs, out_specs=out_specs, check_vma=False)
```

profile of v0, /device:TPU:0, one launch (start us, length us, event | category | flops | bytes accessed | tf_op | source)
XLA Modules:
  0.0 109.3 jit_solution(14182346322377410926)
XLA Ops:
  1.6 2.1 %reshape.1986 = f32[4,4,2,64,128,1]{4,3,2,1,0,5:T(8,128)S(1)} reshape(f32[4,4,2,8192]{3,2,1,0:T(2,128)} %param.7) | data formatting | bytes 2097152 | tf_op jit(solution)/shard_map/reshape | solution.py:70
  4.3 1.1 convolution_bitcast_fusion.7
  5.6 1.0 convolution_bitcast_fusion.6
  7.3 0.8 reshape.2011
  8.1 1.0 fusion.154
  9.6 0.7 reshape.1983
  10.5 1.1 %convolution_bitcast_fusion.5 = f32[4,4,2,64,128]{4,3,1,0,2:T(8,128)S(1)} fusion(f32[4,4,2,64,128]{4,3,1,2,0:T(8,128)S(1)} %reshape.1983, f32[1,64,2,64]{3,1,2,0:T(8,128)S(1)} %copy-done.11, f32[1,64,2,64]{3,1,2,0:T(8,128)S(1)} %get-tuple-element.25), kind=kOutput, calls=%fused_computation.10 | convolution fusion | flops 402669568 | bytes 2162688 | tf_op jit(solution)/shard_map/okci,pqcij->pqokj/dot_general | solution.py:82
  11.7 1.0 fusion.5
  13.4 0.7 div.115
  14.1 1.2 %copy.76 = f32[4,2,4,8,4,256]{5,3,2,1,0,4:T(8,128)} copy(f32[4,2,4,8,4,256]{5,4,3,2,1,0:T(4,128)S(1)} %div.115) | data formatting | bytes 2097152 | tf_op jit(solution)/shard_map/div | solution.py:90
  15.3 5.3 %all-to-all-start = ((f32[4,2,4,8,4,256]{5,3,2,1,0,4:T(8,128)}), f32[4,2,4,8,4,256]{5,3,2,1,0,4:T(8,128)S(1)}, u32[]{:S(2)}, u32[]{:S(2)}) async-start(f32[4,2,4,8,4,256]{5,3,2,1,0,4:T(8,128)} %copy.76), calls=%async_computation | async-start | bytes 2097152 | tf_op jit(solution)/shard_map/all_to_all | solution.py:154
  22.3 11.9 %all-to-all-done = f32[4,2,4,8,4,256]{5,3,2,1,0,4:T(8,128)S(1)} async-done(((f32[4,2,4,8,4,256]{5,3,2,1,0,4:T(8,128)}), f32[4,2,4,8,4,256]{5,3,2,1,0,4:T(8,128)S(1)}, u32[]{:S(2)}, u32[]{:S(2)}) %all-to-all-start) | async-done | bytes 1048608 | tf_op jit(solution)/shard_map/all_to_all | solution.py:154
  34.2 1.6 %copy.77 = f32[4,2,4,8,4,256]{5,4,2,1,0,3:T(4,128)} copy(f32[4,2,4,8,4,256]{5,3,2,1,0,4:T(8,128)S(1)} %all-to-all-done) | data formatting | bytes 2097152 | tf_op jit(solution)/shard_map/all_to_all | solution.py:154
  35.8 5.1 %all-to-all-start.1 = ((f32[4,2,4,8,4,256]{5,4,2,1,0,3:T(4,128)}), f32[4,2,4,8,4,256]{5,4,2,1,0,3:T(4,128)S(1)}, u32[]{:S(2)}, u32[]{:S(2)}) async-start(f32[4,2,4,8,4,256]{5,4,2,1,0,3:T(4,128)} %copy.77), calls=%async_computation.1 | async-start | bytes 2097152 | tf_op jit(solution)/shard_map/all_to_all | solution.py:155
  41.5 0.7 fusion.123
  42.8 0.7 fusion.73
  44.1 0.8 broadcast_compare_fusion.17
  44.9 7.5 %broadcast_compare_fusion.15 = (pred[256,512]{0,1:T(8,128)(4,1)S(1)}, pred[256,512]{0,1:T(8,128)(4,1)S(1)}, pred[256,512]{0,1:T(8,128)(4,1)S(1)}, pred[256,512]{...) fusion(s32[256]{0:T(256)S(1)} %get-tuple-element.58, ...), kind=kLoop, calls=%fused_computation.103 | loop fusion | flops 3670016 | bytes 2234368 | tf_op jit(solution)/shard_map/eq | solution.py:128
  52.4 15.1 %all-to-all-done.1 = f32[4,2,4,8,4,256]{5,4,2,1,0,3:T(4,128)S(1)} async-done(((f32[4,2,4,8,4,256]{5,4,2,1,0,3:T(4,128)}), f32[4,2,4,8,4,256]{5,4,2,1,0,3:T(4,128)S(1)}, u32[]{:S(2)}, u32[]{:S(2)}) %all-to-all-start.1) | async-done | bytes 1048608 | tf_op jit(solution)/shard_map/all_to_all | solution.py:155
  68.2 1.8 %convolution_bitcast_fusion.3 = f32[4,2,256,4,32]{2,4,1,3,0:T(8,128)S(1)} fusion(f32[4,2,4,32,256,1]{4,3,1,2,0,5:T(8,128)S(1)} %reshape.1997, f32[1,32,2,32]{3,1,2,0:T(8,128)} %get-tuple-element.33, f32[1,32,2,32]{3,1,2,0:T(8,128)} %get-tuple-element.34), kind=kOutput, calls=%fused_computation.8 | convolution fusion | flops 201330688 | bytes 2113536 | tf_op jit(solution)/shard_map/okcm,qcimb->qobik/dot_general | solution.py:96
  71.0 2.6 %fusion.3 = f32[4,2,256,4,32]{2,3,1,4,0:T(4,128)S(1)} fusion(f32[4,2,256,4,32,1]{2,4,1,3,0,5:T(8,128)S(1)} %maximum_bitcast_fusion.2, f32[1,4,2,4]{3,1,2,0:T(4,128)S(1)} %copy-done.18, f32[1,4,2,4]{3,1,2,0:T(4,128)S(1)} %copy-done.17), kind=kOutput, calls=%fused_computation.7 | convolution fusion | flops 25428032 | bytes 2097408 | tf_op jit(solution)/shard_map/olci,qcbik->qoblk/dot_general | solution.py:99
  74.0 1.3 %fusion.42 = f32[128,256,4]{1,2,0:T(4,128)S(1)} fusion(f32[4,4,128]{1,0,2:T(4,128)S(1)} %copy.86, f32[4,1,256,128]{2,3,1,0:T(8,128)S(1)} %get-tuple-element.17), kind=kOutput, calls=%fused_computation.80 | convolution fusion | flops 6291456 | bytes 1056768 | tf_op jit(solution)/shard_map/bcf,crf->rbf/dot_general | solution.py:105
  75.3 1.3 %fusion.43 = f32[128,256,4]{1,2,0:T(4,128)S(1)} fusion(f32[4,4,128]{1,0,2:T(4,128)S(1)} %copy.86, f32[4,1,256,128]{2,3,1,0:T(8,128)S(1)} %get-tuple-element.18), kind=kOutput, calls=%fused_computation.81 | convolution fusion | flops 6291456 | bytes 1056768 | tf_op jit(solution)/shard_map/bcf,crf->rbf/dot_general | solution.py:108
  76.7 1.4 %fusion.7 = f32[256,4,128]{0,1,2:T(4,128)S(1)} fusion(f32[128,256,4]{1,2,0:T(4,128)S(1)} %fusion.42, f32[4,4,128]{1,0,2:T(4,128)S(1)} %copy.88, f32[4,1,256,128]{2,3,1,0:T(8,128)S(1)} %get-tuple-element.18), kind=kOutput, calls=%fused_computation.21 | convolution fusion | flops 6422528 | bytes 1581056 | tf_op jit(solution)/shard_map/bcf,crf->rbf/dot_general | solution.py:107
  78.2 1.4 %fusion.6 = f32[256,4,128]{0,1,2:T(4,128)S(1)} fusion(f32[128,256,4]{1,2,0:T(4,128)S(1)} %fusion.43, f32[4,4,128]{1,0,2:T(4,128)S(1)} %copy.88, f32[4,1,256,128]{2,3,1,0:T(8,128)S(1)} %get-tuple-element.17), kind=kOutput, calls=%fused_computation.19 | convolution fusion | flops 6422528 | bytes 1581056 | tf_op jit(solution)/shard_map/bcf,crf->rbf/dot_general | solution.py:110
  79.7 1.3 %collective-permute-start = (f32[2,16,512]{1,2,0:T(8,128)S(1)}, f32[2,16,512]{1,2,0:T(8,128)S(1)}, u32[]{:S(2)}, u32[]{:S(2)}) collective-permute-start(f32[2,16,512]{1,2,0:T(8,128)S(1)} %fusion.40), channel_id=1, source_target_pairs={{1,0},{2,1},{3,2},{4,3},{5,4},{6,5},{7,6},{8,7},{9,8},{10,9},{11,1... | collective-permute-start | bytes 196616 | tf_op jit(solution)/shard_map/ppermute | solution.py:18
  81.2 13.9 %collective-permute-done = f32[2,16,512]{1,2,0:T(8,128)S(1)} collective-permute-done((f32[2,16,512]{1,2,0:T(8,128)S(1)}, f32[2,16,512]{1,2,0:T(8,128)S(1)}, u32[]{:S(2)}, u32[]{:S(2)}) %collective-permute-start) | collective-permute-done | bytes 65568 | tf_op jit(solution)/shard_map/ppermute | solution.py:18
  95.3 4.7 %fusion.24 = f32[2,256,512]{1,2,0:T(8,128)S(1)} fusion(f32[1,256,512]{1,2,0:T(8,128)S(1)} %bitcast.193, f32[1,256,512]{1,2,0:T(8,128)S(1)} %bitcast.190, f32[2,272,512]{1,2,0:T(8,128)S(1)} %pad_maximum_fusion, pred[256,512]{0,1:T(8,128)(4,1)S(1)} %copy-done.8, pred[256,512]{0,1:T(8,128)(4,1)S(1)} %copy-done.7, pred[256,512]{0,1:T(8,128)(4,1)S(1)} %copy-done.6, ...), kind=kLoop, calls=%fused_computation.38 | loop fusion | flops 4718592 | bytes 21102592 | tf_op jit(solution)/shard_map/jit(_where)/select_n | solution.py:128
  100.1 2.1 %fusion.38 = (f32[1,256,512]{1,2,0:T(8,128)S(1)}, f32[1,256,512]{1,2,0:T(8,128)S(1)}) fusion(f32[2,256,512]{1,2,0:T(8,128)S(1)} %fusion.24, f32[512]{0:T(512)S(1)} %multiply_multiply_fusion, f32[256]{0:T(256)S(1)} %copy-done.22), kind=kLoop, calls=%fused_computation.61 | loop fusion | flops 917504 | bytes 2100224 | tf_op jit(solution)/shard_map/sub | solution.py:60
  102.9 1.7 %convolution_bitcast_fusion.1 = f32[2,256,16,32]{1,2,0,3:T(8,128)S(1)} fusion(f32[2,256,16,32,1]{1,3,2,0,4:T(8,128)S(1)} %fusion.25, f32[1,16,2,16]{3,1,2,0:T(8,128)S(1)} %copy-done.14, f32[1,16,2,16]{3,1,2,0:T(8,128)S(1)} %get-tuple-element.35), kind=kOutput, calls=%fused_computation.4 | convolution fusion | flops 100664320 | bytes 2101248 | tf_op jit(solution)/shard_map/okci,cbij->obkj/dot_general | solution.py:136
  105.6 1.7 %fusion.1 = f32[2,256,32,16]{1,2,0,3:T(8,128)S(1)} fusion(f32[2,256,16,32,1]{1,2,0,3,4:T(8,128)S(1)} %maximum_bitcast_fusion.3, f32[1,32,2,32]{3,1,2,0:T(8,128)S(1)} %copy-done.13, f32[1,32,2,32]{3,1,2,0:T(8,128)S(1)} %copy-done.12), kind=kOutput, calls=%fused_computation.3 | convolution fusion | flops 201592832 | bytes 2113536 | tf_op jit(solution)/shard_map/olcj,cbkj->oblk/dot_general | solution.py:139
  108.0 1.3 %copy.96 = f32[2,256,512]{2,1,0:T(8,128)} copy(f32[2,256,512]{1,2,0:T(8,128)S(1)} %bitcast.195) | data formatting | bytes 2097152 | tf_op jit(solution)/shard_map/div | solution.py:142
  (104 shorter events, 12.4 us)
Async XLA Ops:
  9.6 0.8 copy-start.11
  15.3 6.9 %copy-start.26 = (s32[4]{0:T(128)S(1)}, s32[4]{0:T(128)}, u32[]{:S(2)}) copy-start(s32[4]{0:T(128)} %param.10) | copy-start | bytes 52
  15.3 7.0 %copy-start.19 = (f32[2,4,4,128]{3,2,1,0:T(4,128)S(1)}, f32[2,4,4,128]{3,2,1,0:T(4,128)}, u32[]{:S(2)}) copy-start(f32[2,4,4,128]{3,2,1,0:T(4,128)} %param.9) | copy-start | bytes 49156
  15.3 18.9 %all-to-all-start = ((f32[4,2,4,8,4,256]{5,3,2,1,0,4:T(8,128)}), f32[4,2,4,8,4,256]{5,3,2,1,0,4:T(8,128)S(1)}, u32[]{:S(2)}, u32[]{:S(2)}) async-start(f32[4,2,4,8,4,256]{5,3,2,1,0,4:T(8,128)} %copy.76), calls=%async_computation | async-start | bytes 2097152 | tf_op jit(solution)/shard_map/all_to_all | solution.py:154
  35.8 7.6 %copy-start.25 = (f32[256]{0:T(256)S(1)}, f32[256]{0:T(256)}, u32[]{:S(2)}) copy-start(f32[256]{0:T(256)} %param.11) | copy-start | bytes 3076
  35.8 8.2 %copy-start.23 = (s32[256]{0:T(256)S(1)}, s32[256]{0:T(256)}, u32[]{:S(2)}) copy-start(s32[256]{0:T(256)} %param.12) | copy-start | bytes 3076
  35.8 9.0 %copy-start.24 = (s32[256]{0:T(256)S(1)}, s32[256]{0:T(256)}, u32[]{:S(2)}) copy-start(s32[256]{0:T(256)} %param.13) | copy-start | bytes 3076
  35.8 31.7 %all-to-all-start.1 = ((f32[4,2,4,8,4,256]{5,4,2,1,0,3:T(4,128)}), f32[4,2,4,8,4,256]{5,4,2,1,0,3:T(4,128)S(1)}, u32[]{:S(2)}, u32[]{:S(2)}) async-start(f32[4,2,4,8,4,256]{5,4,2,1,0,3:T(4,128)} %copy.77), calls=%async_computation.1 | async-start | bytes 2097152 | tf_op jit(solution)/shard_map/all_to_all | solution.py:155
  68.2 1.9 %copy-start.20 = (f32[4,32]{1,0:T(4,128)S(1)}, f32[4,32]{1,0:T(4,128)}, u32[]{:S(2)}) copy-start(f32[4,32]{1,0:T(4,128)} %get-tuple-element.75) | copy-start | bytes 1540
  68.2 1.9 %copy-start.21 = (f32[4,32]{1,0:T(4,128)S(1)}, f32[4,32]{1,0:T(4,128)}, u32[]{:S(2)}) copy-start(f32[4,32]{1,0:T(4,128)} %get-tuple-element.76) | copy-start | bytes 1540
  70.3 0.7 copy-start.17
  70.3 0.7 copy-start.18
  79.7 15.4 %collective-permute-start = (f32[2,16,512]{1,2,0:T(8,128)S(1)}, f32[2,16,512]{1,2,0:T(8,128)S(1)}, u32[]{:S(2)}, u32[]{:S(2)}) collective-permute-start(f32[2,16,512]{1,2,0:T(8,128)S(1)} %fusion.40), channel_id=1, source_target_pairs={{1,0},{2,1},{3,2},{4,3},{5,4},{6,5},{7,6},{8,7},{9,8},{10,9},{11,1... | collective-permute-start | bytes 196616 | tf_op jit(solution)/shard_map/ppermute | solution.py:18
  81.1 14.2 %copy-start = (pred[256,512]{0,1:T(8,128)(4,1)S(1)}, pred[256,512]{0,1:T(8,128)(4,1)}, u32[]{:S(2)}) copy-start(pred[256,512]{0,1:T(8,128)(4,1)} %get-tuple-element.44) | copy-start | bytes 393220
  81.1 14.2 %copy-start.1 = (pred[256,512]{0,1:T(8,128)(4,1)S(1)}, pred[256,512]{0,1:T(8,128)(4,1)}, u32[]{:S(2)}) copy-start(pred[256,512]{0,1:T(8,128)(4,1)} %get-tuple-element.45) | copy-start | bytes 393220
  81.1 14.2 %copy-start.2 = (pred[256,512]{0,1:T(8,128)(4,1)S(1)}, pred[256,512]{0,1:T(8,128)(4,1)}, u32[]{:S(2)}) copy-start(pred[256,512]{0,1:T(8,128)(4,1)} %get-tuple-element.46) | copy-start | bytes 393220
  81.1 14.2 %copy-start.3 = (pred[256,512]{0,1:T(8,128)(4,1)S(1)}, pred[256,512]{0,1:T(8,128)(4,1)}, u32[]{:S(2)}) copy-start(pred[256,512]{0,1:T(8,128)(4,1)} %get-tuple-element.47) | copy-start | bytes 393220
  81.1 14.2 %copy-start.4 = (pred[256,512]{0,1:T(8,128)(4,1)S(1)}, pred[256,512]{0,1:T(8,128)(4,1)}, u32[]{:S(2)}) copy-start(pred[256,512]{0,1:T(8,128)(4,1)} %get-tuple-element.48) | copy-start | bytes 393220
  81.1 14.2 %copy-start.5 = (pred[256,512]{0,1:T(8,128)(4,1)S(1)}, pred[256,512]{0,1:T(8,128)(4,1)}, u32[]{:S(2)}) copy-start(pred[256,512]{0,1:T(8,128)(4,1)} %get-tuple-element.49) | copy-start | bytes 393220
  81.1 14.2 %copy-start.6 = (pred[256,512]{0,1:T(8,128)(4,1)S(1)}, pred[256,512]{0,1:T(8,128)(4,1)}, u32[]{:S(2)}) copy-start(pred[256,512]{0,1:T(8,128)(4,1)} %get-tuple-element.50) | copy-start | bytes 393220
  81.1 14.2 %copy-start.7 = (pred[256,512]{0,1:T(8,128)(4,1)S(1)}, pred[256,512]{0,1:T(8,128)(4,1)}, u32[]{:S(2)}) copy-start(pred[256,512]{0,1:T(8,128)(4,1)} %get-tuple-element.51) | copy-start | bytes 393220
  81.1 14.2 %copy-start.8 = (pred[256,512]{0,1:T(8,128)(4,1)S(1)}, pred[256,512]{0,1:T(8,128)(4,1)}, u32[]{:S(2)}) copy-start(pred[256,512]{0,1:T(8,128)(4,1)} %get-tuple-element.52) | copy-start | bytes 393220
  81.1 14.2 %copy-start.9 = (pred[256,512]{0,1:T(8,128)(4,1)S(1)}, pred[256,512]{0,1:T(8,128)(4,1)}, u32[]{:S(2)}) copy-start(pred[256,512]{0,1:T(8,128)(4,1)} %get-tuple-element.53) | copy-start | bytes 393220
  95.3 4.8 %copy-start.22 = (f32[256]{0:T(256)S(1)}, f32[256]{0:T(256)}, u32[]{:S(2)}) copy-start(f32[256]{0:T(256)} %broadcast_multiply_fusion.4) | copy-start | bytes 3076
  100.1 2.2 %copy-start.10 = (pred[256,16,32]{0,2,1:T(8,128)(4,1)S(1)}, pred[256,16,32]{0,2,1:T(8,128)(4,1)}, u32[]{:S(2)}) copy-start(pred[256,16,32]{0,2,1:T(8,128)(4,1)} %broadcast_compare_fusion.17) | copy-start | bytes 393220
  102.2 0.7 copy-start.14
  102.4 2.2 %copy-start.15 = (f32[16,32]{0,1:T(8,128)S(1)}, f32[16,32]{0,1:T(8,128)}, u32[]{:S(2)}) copy-start(f32[16,32]{0,1:T(8,128)} %get-tuple-element.81) | copy-start | bytes 6148
  102.5 2.2 %copy-start.16 = (f32[16,32]{0,1:T(8,128)S(1)}, f32[16,32]{0,1:T(8,128)}, u32[]{:S(2)}) copy-start(f32[16,32]{0,1:T(8,128)} %get-tuple-element.82) | copy-start | bytes 6148
  104.9 0.8 copy-start.12
  104.9 0.8 copy-start.13
where the time goes:
time: 110 us; the launch traced here: 109 us
  waiting for transfers between devices  40.9 us (37%)
  other arithmetic  24.6 us (22%)
  matrix products  17.5 us (16%)
  local copies, waits for them, and re-layouts  13.9 us (13%)
  starting transfers between devices  11.7 us (11%)
    all_to_all x1, waiting for transfers between devices, local(): lax.all_to_all(layout, 'az', split_axis=3, concat_axis=3, tiled=True)  15.1 us
    ppermute x1, waiting for transfers between devices, passed_along(): return lax.ppermute(value, axis, pairs)  13.9 us
    all_to_all x1, waiting for transfers between devices, local(): lax.all_to_all(layout, 'rg', split_axis=4, concat_axis=4, tiled=True)  11.9 us
    eq x1, other arithmetic, azimuth_focus(): migrated = jnp.where((migration_shift == offset)[None], window, migrated)  7.54 us
    all_to_all x1, starting transfers between devices, local(): lax.all_to_all(layout, 'rg', split_axis=4, concat_axis=4, tiled=True)  5.3 us
    all_to_all x1, starting transfers between devices, local(): lax.all_to_all(layout, 'az', split_axis=3, concat_axis=3, tiled=True)  5.07 us
    select_n x1, other arithmetic, azimuth_focus(): migrated = jnp.where((migration_shift == offset)[None], window, migrated)  4.73 us
    sub x6, other arithmetic, complex_mul(): real_part * factor_real - imag_part * factor_imag  3.09 us
  transfers between devices with their start and end apart: 3, of which 3 were waited for; matrix products, arithmetic and copies ran while one was open for 12% of the time, Pallas kernels for 0%

commit v1 on v0

--- a/solution.py
+++ b/solution.py
@@ -1,11 +1,18 @@
+import functools
 import math
 
 import jax
 import jax.numpy as jnp
+import ml_dtypes
+import numpy as np
 from jax import lax
+from jax.experimental import pallas as pl
+from jax.experimental.pallas import tpu as pltpu
 from jax.sharding import PartitionSpec as P
 
 MIG = 16
+LANES = 128
+HALO_ROWS = 8
 
 
 highest = lax.Precision.HIGHEST
@@ -142,7 +149,7 @@
     return focused_image.reshape(2, bin_count, length) / math.sqrt(length)
 
 
-def local(
+def plain_local(
     raw_echoes, chirp_spectrum, reconstruction, delays, azimuth_rate, band_halfwidth, migration
 ):
     compressed = range_focus(raw_echoes, chirp_spectrum)
@@ -172,6 +179,449 @@
     return azimuth_focus(unfolded, azimuth_rate, band_halfwidth, migration)
 
 
+def split_constant(values):
+    high = values.astype(ml_dtypes.bfloat16)
+    low = (values - high.astype(np.float64)).astype(ml_dtypes.bfloat16)
+    return np.stack([high, low])
+
+
+def roots(rows, columns, length, direction):
+    turns = (rows[:, None] * columns[None, :]) % length
+    angles = 2.0 * np.pi / length * turns
+    return np.cos(angles), direction * np.sin(angles)
+
+
+def left_matrix(cosine, sine):
+    return np.stack([np.stack([cosine, -sine], 1), np.stack([sine, cosine], 1)], 0)
+
+
+def right_matrix(cosine, sine):
+    return np.stack([np.stack([cosine, sine], 1), np.stack([-sine, cosine], 1)], 0)
+
+
+def split(values):
+    high = values.astype(jnp.bfloat16)
+    low = (values - high.astype(jnp.float32)).astype(jnp.bfloat16)
+    return high, low
+
+
+def dot(a, b):
+    return jnp.dot(a, b, preferred_element_type=jnp.float32)
+
+
+def dot_right(values, matrix):
+    high, low = split(values)
+    return dot(high, matrix[0]) + (dot(low, matrix[0]) + dot(high, matrix[1]))
+
+
+def dot_left(matrix, values):
+    high, low = split(values)
+    return dot(matrix[0], high) + (dot(matrix[1], high) + dot(matrix[0], low))
+
+
+def cos_sin_turns(turns):
+    quarter = jnp.floor(turns * 4.0 + 0.5)
+    theta = (turns - quarter * 0.25) * (2.0 * math.pi)
+    square = theta * theta
+    cosine = 1.0 + square * (
+        -0.5 + square * (1.0 / 24 + square * (-1.0 / 720 + square * (1.0 / 40320)))
+    )
+    sine = theta * (
+        1.0
+        + square
+        * (-1.0 / 6 + square * (1.0 / 120 + square * (-1.0 / 5040 + square * (1.0 / 362880))))
+    )
+    index = quarter.astype(jnp.int32)
+    odd = (index & 1) == 1
+    cos_negative = ((index + 1) & 2) == 2
+    sin_negative = (index & 2) == 2
+    cos_size = jnp.where(odd, sine, cosine)
+    sin_size = jnp.where(odd, cosine, sine)
+    return (
+        jnp.where(cos_negative, -cos_size, cos_size),
+        jnp.where(sin_negative, -sin_size, sin_size),
+    )
+
+
+def range_kernel(
+    sizes, x_ref, chirp_ref, first_ref, twiddle_ref, fwd_ref, inv_ref, last_ref, halo_ref, out_ref
+):
+    pulses, channels, lead, devices = sizes
+    tw_r = jnp.concatenate([twiddle_ref[0]] * channels, axis=0)
+    tw_i = jnp.concatenate([twiddle_ref[1]] * channels, axis=0)
+    chirp_r = jnp.concatenate([chirp_ref[0]] * channels, axis=0)
+    chirp_i = jnp.concatenate([chirp_ref[1]] * channels, axis=0)
+    lane = lax.broadcasted_iota(jnp.int32, (2 * lead, LANES), 1)
+    groups = pulses * channels * MIG // LANES
+    per_group = LANES // MIG
+    packs = [jnp.zeros((2 * lead, LANES), jnp.float32) for _ in range(groups)]
+    for p in range(pulses):
+        x = jnp.concatenate([x_ref[p * channels + c] for c in range(channels)], axis=1)
+        y = dot_left(first_ref, x)
+        y = jnp.concatenate([y[:, c * LANES : (c + 1) * LANES] for c in range(channels)], axis=0)
+        y = y.reshape(channels, 2, lead, LANES)
+        y_r = y[:, 0].reshape(channels * lead, LANES)
+        y_i = y[:, 1].reshape(channels * lead, LANES)
+        y = jnp.concatenate([y_r * tw_r - y_i * tw_i, y_r * tw_i + y_i * tw_r], axis=1)
+        s = dot_right(y, fwd_ref)
+        s_r, s_i = s[:, :LANES], s[:, LANES:]
+        s = jnp.concatenate(
+            [s_r * chirp_r + s_i * chirp_i, s_i * chirp_r - s_r * chirp_i], axis=1
+        )
+        t = dot_right(s, inv_ref)
+        t_r, t_i = t[:, :LANES], t[:, LANES:]
+        z_r = t_r * tw_r + t_i * tw_i
+        z_i = t_i * tw_r - t_r * tw_i
+        z = [
+            jnp.concatenate(
+                [z_r[c * lead : (c + 1) * lead], z_i[c * lead : (c + 1) * lead]], axis=0
+            )
+            for c in range(channels)
+        ]
+        pairs = channels // 2
+        stacked = jnp.concatenate(
+            [jnp.concatenate([z[2 * k], z[2 * k + 1]], axis=0) for k in range(pairs)], axis=1
+        )
+        w = dot_left(last_ref, stacked)
+        for k in range(pairs):
+            row = (p * pairs + k) * 8
+            out_ref[:, row : row + 8, :] = w[:, k * LANES : (k + 1) * LANES].reshape(
+                devices, 8, LANES
+            )
+        for c in range(channels):
+            signal = p * channels + c
+            g, place = signal // per_group, signal % per_group
+            moved = z[c] if place == 0 else pltpu.roll(z[c], place * MIG, 1)
+            packs[g] = jnp.where(lane // MIG == place, moved, packs[g])
+    w = dot_left(halo_ref, jnp.concatenate(packs, axis=1))
+    row = lax.broadcasted_iota(jnp.int32, (devices * HALO_ROWS, LANES), 0) % HALO_ROWS
+    total = w[:, :LANES]
+    for g in range(1, groups):
+        total = jnp.where(row // 2 == g, w[:, g * LANES : (g + 1) * LANES], total)
+    out_ref[:, pulses * channels * 4 :, :] = total.reshape(devices, HALO_ROWS, LANES)
+
+
+def exchange_kernel(devices, inner, send_ref, recv_ref, local_sem, send_sems, recv_sems):
+    mine = lax.axis_index("az") * inner + lax.axis_index("rg")
+    barrier = pltpu.get_barrier_semaphore()
+
+    def place(index):
+        return (lax.div(index, inner), lax.rem(index, inner))
+
+    for k in range(1, devices):
+        pl.semaphore_signal(
+            barrier,
+            inc=1,
+            device_id=place(lax.rem(mine + k, devices)),
+            device_id_type=pl.DeviceIdType.MESH,
+        )
+    own = pltpu.make_async_copy(send_ref.at[mine], recv_ref.at[mine], local_sem)
+    own.start()
+    pl.semaphore_wait(barrier, devices - 1)
+    copies = []
+    for k in range(devices // 2, 0, -1):
+        for step in sorted({k, devices - k}):
+            target = lax.rem(mine + step, devices)
+            copy = pltpu.make_async_remote_copy(
+                src_ref=send_ref.at[target],
+                dst_ref=recv_ref.at[mine],
+                send_sem=send_sems.at[step],
+                recv_sem=recv_sems.at[step],
+                device_id=place(target),
+                device_id_type=pl.DeviceIdType.MESH,
+            )
+            copy.start()
+            copies.append(copy)
+    own.wait()
+    for copy in copies:
+        copy.wait()
+
+
+def azimuth_kernel(
+    sizes,
+    recv_ref,
+    reconstruction_ref,
+    delays_ref,
+    rate_ref,
+    band_ref,
+    migration_ref,
+    doppler_ref,
+    halo_doppler_ref,
+    final_hbm,
+    out_ref,
+    spectra,
+    unfolded,
+    focused,
+    mix,
+    final,
+    final_sem,
+):
+    sources, local_pulses, channels, bins = sizes
+    pulses = sources * local_pulses
+    block = local_pulses * channels * 4 + HALO_ROWS
+    length = channels * pulses
+    load = pltpu.make_async_copy(final_hbm, final, final_sem)
+    load.start()
+
+    row = lax.broadcasted_iota(jnp.int32, (channels * channels, pulses), 0) % channels
+    frequency = lax.broadcasted_iota(jnp.int32, (channels * channels, pulses), 1)
+    delay = jnp.zeros_like(row)
+    for c in range(channels):
+        delay = jnp.where(row == c, delays_ref[c], delay)
+    turns = lax.rem(frequency * delay, pulses).astype(jnp.float32) * (1.0 / pulses)
+    align_r, align_i = cos_sin_turns(turns)
+    rec_r, rec_i = reconstruction_ref[0], reconstruction_ref[1]
+    mix[0] = rec_r * align_r - rec_i * align_i
+    mix[1] = rec_r * align_i + rec_i * align_r
+
+    def rows_of(start):
+        return recv_ref[pl.ds(start, sources, stride=block), :]
+
+    for c in range(channels):
+        for half in range(bins // LANES):
+            z = jnp.concatenate(
+                [
+                    rows_of(p * channels * 4 + c * 4 + part * 2 + half)
+                    for part in range(2)
+                    for p in range(local_pulses)
+                ],
+                axis=0,
+            )
+            spectra[c, half * LANES : (half + 1) * LANES, :] = dot_right(z.T, doppler_ref)
+    groups = local_pulses * channels * MIG // LANES
+    per_group = LANES // (MIG * channels)
+    h = jnp.concatenate(
+        [
+            rows_of(local_pulses * channels * 4 + g * 2 + part)
+            for g in range(groups)
+            for part in range(2)
+        ],
+        axis=0,
+    ).T
+    step = channels * MIG
+    halo = dot_right(h[:step], halo_doppler_ref.at[0])
+    for k in range(1, per_group):
+        halo = halo + dot_right(h[k * step : (k + 1) * step], halo_doppler_ref.at[k])
+    for c in range(channels):
+        spectra[c, bins:, :] = halo[c * MIG : (c + 1) * MIG]
+
+    def mix_rows(index, carry):
+        at = pl.ds(pl.multiple_of(index * 8, 8), 8)
+        spec = [spectra[c, at, :] for c in range(channels)]
+        for b in range(channels):
+            total_r = total_i = None
+            for c in range(channels):
+                m = b * channels + c
+                m_r = jnp.broadcast_to(mix[0, m : m + 1, :], (8, pulses))
+                m_i = jnp.broadcast_to(mix[1, m : m + 1, :], (8, pulses))
+                d_r, d_i = spec[c][:, :pulses], spec[c][:, pulses:]
+                r = m_r * d_r - m_i * d_i
+                i = m_r * d_i + m_i * d_r
+                total_r = r if c == 0 else total_r + r
+                total_i = i if c == 0 else total_i + i
+            unfolded[at, b * pulses : (b + 1) * pulses] = total_r
+            unfolded[at, length + b * pulses : length + (b + 1) * pulses] = total_i
+        return carry
+
+    lax.fori_loop(0, (bins + MIG) // 8, mix_rows, 0)
+
+    def focus_band(b, carry):
+        lane = pl.multiple_of(b * LANES, LANES)
+        at_real = pl.ds(lane, LANES)
+        at_imag = pl.ds(pl.multiple_of(length + lane, LANES), LANES)
+        doppler = lax.broadcasted_iota(jnp.int32, (8, LANES), 1) + lane
+        centred = doppler - jnp.where(doppler >= length // 2, length, 0)
+        centred_square = centred * centred
+        distance = jnp.abs(centred)
+        relative = centred.astype(jnp.float32) * (2.0 / length)
+        chirp_turns = relative * relative * (curvature / 2.0)
+        for start in range(0, bins, 8):
+            at = slice(start, start + 8)
+            rate = jnp.broadcast_to(rate_ref[at, :], (8, LANES))
+            band = jnp.broadcast_to(band_ref[at, :], (8, LANES))
+            move = jnp.broadcast_to(migration_ref[at, :], (8, LANES))
+            band_square = band * band
+            reach = move * jnp.minimum(centred_square, band_square) + (band_square >> 1)
+            real = unfolded[at, at_real]
+            imag = unfolded[at, at_imag]
+            bound = band_square
+            for offset in range(1, MIG + 1):
+                moved = reach >= bound
+                window = slice(start + offset, start + offset + 8)
+                real = jnp.where(moved, unfolded[window, at_real], real)
+                imag = jnp.where(moved, unfolded[window, at_imag], imag)
+                bound = bound + band_square
+            cosine, sine = cos_sin_turns(rate * chirp_turns)
+            inside = distance < band
+            focused[at, at_real] = jnp.where(inside, real * cosine - imag * sine, 0.0)
+            focused[at, at_imag] = jnp.where(inside, real * sine + imag * cosine, 0.0)
+        return carry
+
+    lax.fori_loop(0, length // LANES, focus_band, 0)
+    load.wait()
+    image = dot_right(focused[...], final)
+    out_ref[0] = image[:, :length]
+    out_ref[1] = image[:, length:]
+
+
+def fits(pulses, channels, length, devices):
+    local_pulses = pulses // devices
+    signals = local_pulses * channels
+    bins = length // devices
+    lead = length // LANES
+    return (
+        pulses == LANES
+        and length % (LANES * devices) == 0
+        and bins == 2 * LANES
+        and channels % 2 == 0
+        and lead % 8 == 0
+        and devices % 8 == 0
+        and signals * MIG % LANES == 0
+        and LANES % (MIG * channels) == 0
+        and 2 * (signals * MIG // LANES) <= HALO_ROWS
+        and channels * pulses <= 512
+    )
+
+
+def vmem():
+    return pl.BlockSpec(memory_space=pltpu.VMEM)
+
+
+def blocked_local(
+    raw_echoes, chirp_spectrum, reconstruction, delays, azimuth_rate, band_halfwidth, migration
+):
+    local_pulses, channels, _, length = raw_echoes.shape
+    inner = lax.axis_size("rg")
+    devices = lax.axis_size("az") * inner
+    bins = length // devices
+    lead = length // LANES
+    pulses = local_pulses * devices
+    signals = local_pulses * channels
+    doppler_bins = channels * pulses
+    leads = np.arange(lead)
+    lanes = np.arange(LANES)
+
+    first = left_matrix(*roots(leads, leads, lead, -1.0))
+    first = first.transpose(0, 1, 3, 2).reshape(2 * lead, 2 * lead)
+    forward = right_matrix(*roots(lanes, lanes, LANES, -1.0)).reshape(2 * LANES, 2 * LANES)
+    inverse = right_matrix(*roots(lanes, lanes, LANES, 1.0)).reshape(2 * LANES, 2 * LANES)
+    last = left_matrix(*roots(leads, leads, lead, 1.0)) / length
+    pair = np.zeros((devices, 2, 2, 2, 2, 2 * lead))
+    by_device = last.reshape(2, devices, 2, 2 * lead).transpose(1, 0, 2, 3)
+    for s in range(2):
+        pair[:, s, :, :, s, :] = by_device
+    pair = pair.reshape(devices * 8, 4 * lead)
+    halo = np.zeros((devices, HALO_ROWS, 2 * lead))
+    groups = signals * MIG // LANES
+    for g in range(groups):
+        halo[:-1, 2 * g : 2 * g + 2] = by_device[1:, :, 0]
+    halo = halo.reshape(devices * HALO_ROWS, 2 * lead)
+    twiddles = np.stack(roots(leads, lanes, length, -1.0)).astype(np.float32)
+
+    sources = np.arange(devices)
+    bins_f = np.arange(pulses)
+    order = (np.arange(local_pulses)[:, None] + sources[None, :] * local_pulses).reshape(-1)
+    scale = 1.0 / math.sqrt(pulses)
+    to_doppler = right_matrix(*roots(order, bins_f, pulses, -1.0)) * scale
+    to_doppler = to_doppler.reshape(2 * pulses, 2 * pulses)
+    per_group = local_pulses // groups
+    halo_doppler = []
+    for k in range(per_group):
+        by_group = []
+        for g in range(groups):
+            at = sources * local_pulses + g * per_group + k
+            by_group.append(
+                (right_matrix(*roots(at, bins_f, pulses, -1.0)) * scale).reshape(
+                    2 * devices, 2 * pulses
+                )
+            )
+        halo_doppler.append(split_constant(np.concatenate(by_group, axis=0)))
+    halo_doppler = np.stack(halo_doppler)
+    indices = np.arange(doppler_bins)
+    final = right_matrix(*roots(indices, indices, doppler_bins, 1.0)) / math.sqrt(doppler_bins)
+    final = final.reshape(2 * doppler_bins, 2 * doppler_bins)
+
+    x = raw_echoes.reshape(signals, 2, lead, LANES).transpose(0, 2, 1, 3)
+    x = x.reshape(signals, 2 * lead, LANES)
+    chirp = chirp_spectrum.reshape(2, LANES, lead).transpose(0, 2, 1)
+    block = signals * 4 + HALO_ROWS
+    send = pl.pallas_call(
+        functools.partial(range_kernel, (local_pulses, channels, lead, devices)),
+        out_shape=jax.ShapeDtypeStruct((devices, block, LANES), jnp.float32),
+        in_specs=[vmem()] * 8,
+        out_specs=vmem(),
+        compiler_params=pltpu.CompilerParams(vmem_limit_bytes=48 * 1024 * 1024),
+        name="range_compress",
+    )(
+        x,
+        chirp,
+        split_constant(first),
+        twiddles,
+        split_constant(forward),
+        split_constant(inverse),
+        split_constant(pair),
+        split_constant(halo),
+    )
+    received = pl.pallas_call(
+        functools.partial(exchange_kernel, devices, inner),
+        out_shape=jax.ShapeDtypeStruct((devices, block, LANES), jnp.float32),
+        in_specs=[pl.BlockSpec(memory_space=pl.ANY)],
+        out_specs=pl.BlockSpec(memory_space=pl.ANY),
+        scratch_shapes=[
+            pltpu.SemaphoreType.DMA,
+            pltpu.SemaphoreType.DMA((devices,)),
+            pltpu.SemaphoreType.DMA((devices,)),
+        ],
+        compiler_params=pltpu.CompilerParams(collective_id=0, has_side_effects=True),
+        name="exchange",
+    )(send)
+    received = received.reshape(devices * block, LANES)
+    return pl.pallas_call(
+        functools.partial(azimuth_kernel, (devices, local_pulses, channels, bins)),
+        out_shape=jax.ShapeDtypeStruct((2, bins, doppler_bins), jnp.float32),
+        in_specs=[
+            vmem(),
+            vmem(),
+            pl.BlockSpec(memory_space=pltpu.SMEM),
+            vmem(),
+            vmem(),
+            vmem(),
+            vmem(),
+            vmem(),
+            pl.BlockSpec(memory_space=pl.ANY),
+        ],
+        out_specs=vmem(),
+        scratch_shapes=[
+            pltpu.VMEM((channels, bins + MIG, 2 * pulses), jnp.float32),
+            pltpu.VMEM((bins + MIG, 2 * doppler_bins), jnp.float32),
+            pltpu.VMEM((bins, 2 * doppler_bins), jnp.float32),
+            pltpu.VMEM((2, channels * channels, pulses), jnp.float32),
+            pltpu.VMEM((2, 2 * doppler_bins, 2 * doppler_bins), jnp.bfloat16),
+            pltpu.SemaphoreType.DMA,
+        ],
+        compiler_params=pltpu.CompilerParams(vmem_limit_bytes=48 * 1024 * 1024),
+        name="azimuth_focus",
+    )(
+        received,
+        reconstruction.reshape(2, channels * channels, pulses),
+        delays,
+        azimuth_rate.reshape(bins, 1),
+        band_halfwidth.reshape(bins, 1),
+        migration.reshape(bins, 1),
+        split_constant(to_doppler),
+        halo_doppler,
+        split_constant(final),
+    )
+
+
+def local(raw_echoes, chirp_spectrum, reconstruction, *rest):
+    local_pulses, channels, _, length = raw_echoes.shape
+    devices = lax.axis_size("az") * lax.axis_size("rg")
+    if fits(local_pulses * devices, channels, length, devices):
+        return blocked_local(raw_echoes, chirp_spectrum, reconstruction, *rest)
+    return plain_local(raw_echoes, chirp_spectrum, reconstruction, *rest)
+
+
 def solution(mesh):
     in_specs = (
         P(("az", "rg"), None, None, None),

time: 110 us -> 55.7 us (0.51)
  Pallas kernels: 0 us -> 44.7 us
  waiting for transfers between devices: 40.9 us -> 0 us
  other arithmetic: 24.6 us -> 0 us
  matrix products: 17.5 us -> 0 us
  starting transfers between devices: 11.7 us -> 0 us
  local copies, waits for them, and re-layouts: 13.9 us -> 10.4 us
    pallas_call x0 -> x3, Pallas kernels: none -> 44.7 us  [the longest x1 33.1 us: blocked_local(): pl.pallas_call(functools.partial(exchange_kernel, devices, inner), out_sh...]
    all_to_all x2 -> x0, waiting for transfers between devices: 27 us -> none  [the longest x1 15.1 us: local(): lax.all_to_all(layout, 'az', split_axis=3, concat_axis=3, tiled=True)]
    dot_general x12 -> x0, matrix products: 17.5 us -> none  [the longest x1 2.61 us: reconstruct(): jnp.einsum('olci,qcbik->qoblk', dft_matrix(local_pulses, -1.0), sectioned...]
    ppermute x1 -> x0, waiting for transfers between devices: 13.9 us -> none  [passed_along(): return lax.ppermute(value, axis, pairs)]
    all_to_all x2 -> x0, starting transfers between devices: 10.4 us -> none  [the longest x1 5.3 us: local(): lax.all_to_all(layout, 'rg', split_axis=4, concat_axis=4, tiled=True)]
    eq x1 -> x0, other arithmetic: 7.54 us -> none  [azimuth_focus(): migrated = jnp.where((migration_shift == offset)[None], window, migrated)]
    unnamed x54 -> x32, local copies, waits for them, and re-layouts: 1.91 us -> 8.98 us
    select_n x3 -> x0, other arithmetic: 4.93 us -> none  [the longest x1 4.73 us: azimuth_focus(): migrated = jnp.where((migration_shift == offset)[None], window, migrated)]
  transfers between devices with their start and end apart: 3 -> 0, of which waited for: 3 -> 0; matrix products, arithmetic and copies ran while one was open for 12% -> 0% of each run, Pallas kernels for 0% -> 0%
where the time goes in v1:
time: 55.7 us; the launch traced here: 55.2 us
  Pallas kernels  44.7 us (80%)
  local copies, waits for them, and re-layouts  10.4 us (19%)
    pallas_call x1, Pallas kernels, blocked_local(): pl.pallas_call(functools.partial(exchange_kernel, devices, inner), out_sh...  33.1 us
    unnamed x32, local copies, waits for them, and re-layouts  8.98 us
    pallas_call x1, Pallas kernels, blocked_local(): pl.pallas_call(functools.partial(azimuth_kernel, (devices, local_pulses,...  7.92 us
    pallas_call x1, Pallas kernels, blocked_local(): pl.pallas_call(functools.partial(range_kernel, (local_pulses, channels, l...  3.63 us

profile of v1, /device:TPU:0, one launch (start us, length us, event | category | flops | bytes accessed | tf_op | source)
XLA Modules:
  0.0 55.2 jit_solution(5892918364365862937)
XLA Ops:
  0.0 1.0 %reshape.26 = f32[2,128,64]{2,1,0:T(8,128)S(1)} reshape(f32[2,8192]{1,0:T(2,128)} %param.17) | data formatting | bytes 131072 | tf_op jit(solution)/shard_map/reshape | solution.py:546
  1.0 0.1 copy.19
  1.1 0.0 copy-start.2
  1.1 1.2 %copy-done.2 = f32[4,4,2,8192]{3,2,1,0:T(2,128)S(1)} copy-done((f32[4,4,2,8192]{3,2,1,0:T(2,128)S(1)}, f32[4,4,2,8192]{3,2,1,0:T(2,128)}, u32[]{:S(2)}) %copy-start.2) | copy-done | bytes 1048600
  2.3 0.0 copy-start.3
  2.3 0.9 %copy-done.3 = bf16[2,256,256]{2,1,0:T(8,128)(2,1)S(1)} copy-done((bf16[2,256,256]{2,1,0:T(8,128)(2,1)S(1)}, bf16[2,256,256]{2,1,0:T(8,128)(2,1)}, u32[]{:S(2)}) %copy-start.3) | copy-done | bytes 262168
  3.2 0.0 copy-start.4
  3.2 0.9 %copy-done.4 = bf16[2,256,256]{2,1,0:T(8,128)(2,1)S(1)} copy-done((bf16[2,256,256]{2,1,0:T(8,128)(2,1)S(1)}, bf16[2,256,256]{2,1,0:T(8,128)(2,1)}, u32[]{:S(2)}) %copy-start.4) | copy-done | bytes 262168
  4.2 0.9 %copy-done.5 = bf16[2,256,256]{2,1,0:T(8,128)(2,1)S(1)} copy-done((bf16[2,256,256]{2,1,0:T(8,128)(2,1)S(1)}, bf16[2,256,256]{2,1,0:T(8,128)(2,1)}, u32[]{:S(2)}) %copy-start.5) | copy-done | bytes 262168
  5.1 0.9 %copy-done.8 = bf16[2,256,128]{2,1,0:T(8,128)(2,1)S(1)} copy-done((bf16[2,256,128]{2,1,0:T(8,128)(2,1)S(1)}, bf16[2,256,128]{2,1,0:T(8,128)(2,1)}, u32[]{:S(2)}) %copy-start.8) | copy-done | bytes 131096
  6.0 0.8 %copy-done.9 = bf16[2,128,128]{2,1,0:T(8,128)(2,1)S(1)} copy-done((bf16[2,128,128]{2,1,0:T(8,128)(2,1)S(1)}, bf16[2,128,128]{2,1,0:T(8,128)(2,1)}, u32[]{:S(2)}) %copy-start.9) | copy-done | bytes 65560
  6.9 0.8 %copy-done.10 = f32[2,64,128]{2,1,0:T(8,128)S(1)} copy-done((f32[2,64,128]{2,1,0:T(8,128)S(1)}, f32[2,64,128]{2,1,0:T(8,128)}, u32[]{:S(2)}) %copy-start.10) | copy-done | bytes 65560
  7.7 3.6 %range_compress.1.send_ref = f32[32,72,128]{2,1,0:T(8,128)S(1)} custom-call(f32[16,128,128]{2,1,0:T(8,128)S(1)} %bitcast.12, f32[2,64,128]{2,1,0:T(8,128)S(1)} %bitcast.13, bf16[2,128,128]{2,1,0:T(8,128)(2,1)S(1)} %copy-done.9, f32[2,64,128]{2,1,0:T(8,128)S(1)} %copy-done.10, bf16[2,256,256]{2,1,0:T(8,128)(2,1)S(1)} %copy-done.3, ...), custom_call_target="tpu_custom_call" | custom-call | tf_op jit(solution)/shard_map/range_compress/pallas_call | solution.py:548
  11.4 0.0 copy-start
  11.4 1.0 %copy-done = f32[32,72,128]{2,1,0:T(8,128)} copy-done((f32[32,72,128]{2,1,0:T(8,128)}, f32[32,72,128]{2,1,0:T(8,128)S(1)}, u32[]{:S(2)}) %copy-start) | copy-done | bytes 1179672
  12.4 0.0 copy-start.7
  12.4 0.0 copy-start.11
  12.4 0.0 copy-start.12
  12.4 33.1 %exchange.1 = f32[32,72,128]{2,1,0:T(8,128)} custom-call(f32[32,72,128]{2,1,0:T(8,128)} %copy-done), custom_call_target="tpu_custom_call" | custom-call | tf_op jit(solution)/shard_map/exchange/pallas_call | solution.py:565
  45.6 0.0 copy-done.13
  45.6 0.1 copy.20.rate_ref
  45.7 0.0 copy-done.14
  45.7 0.1 copy.21.band_ref
  45.9 0.0 copy-done.15
  45.9 0.1 copy.22.migration_ref
  46.0 0.0 copy-done.6
  46.0 0.0 copy-done.7
  46.0 0.0 copy-done.11
  46.0 0.0 copy-done.12
  46.1 0.0 copy-start.1
  46.1 1.3 %copy-done.1 = f32[32,72,128]{2,1,0:T(8,128)S(1)} copy-done((f32[32,72,128]{2,1,0:T(8,128)S(1)}, f32[32,72,128]{2,1,0:T(8,128)}, u32[]{:S(2)}) %copy-start.1) | copy-done | bytes 1179672
  47.3 7.9 %azimuth_focus.1 = f32[2,256,512]{2,1,0:T(8,128)} custom-call(f32[2304,128]{1,0:T(8,128)S(1)} %bitcast.11, f32[2,16,128]{2,1,0:T(8,128)S(1)} %bitcast.14, s32[4]{0:T(128)S(1)} %copy-done.12, f32[256,1]{1,0:T(8,128)S(1)} %copy.20.rate_ref, s32[256,1]{1,0:T(8,128)S(1)} %copy.21.band_ref, s32[256,1]{1,0:T(8,128)S(1)} %copy.22.migration_ref, ...), custom_call_target="tpu_custom_call" | custom-call | tf_op jit(solution)/shard_map/azimuth_focus/pallas_call | solution.py:579
  (8 shorter events, 0.0 us)
Async XLA Ops:
  1.1 1.2 %copy-start.2 = (f32[4,4,2,8192]{3,2,1,0:T(2,128)S(1)}, f32[4,4,2,8192]{3,2,1,0:T(2,128)}, u32[]{:S(2)}) copy-start(f32[4,4,2,8192]{3,2,1,0:T(2,128)} %param.16) | copy-start | bytes 3145732
  2.3 0.9 %copy-start.3 = (bf16[2,256,256]{2,1,0:T(8,128)(2,1)S(1)}, bf16[2,256,256]{2,1,0:T(8,128)(2,1)}, u32[]{:S(2)}) copy-start(bf16[2,256,256]{2,1,0:T(8,128)(2,1)} %constant.20.clone.fwd_ref) | copy-start | bytes 786436
  3.2 0.9 %copy-start.4 = (bf16[2,256,256]{2,1,0:T(8,128)(2,1)S(1)}, bf16[2,256,256]{2,1,0:T(8,128)(2,1)}, u32[]{:S(2)}) copy-start(bf16[2,256,256]{2,1,0:T(8,128)(2,1)} %constant.21.clone.inv_ref) | copy-start | bytes 786436
  4.2 0.9 %copy-start.5 = (bf16[2,256,256]{2,1,0:T(8,128)(2,1)S(1)}, bf16[2,256,256]{2,1,0:T(8,128)(2,1)}, u32[]{:S(2)}) copy-start(bf16[2,256,256]{2,1,0:T(8,128)(2,1)} %constant.22.clone.last_ref) | copy-start | bytes 786436
  5.1 0.9 %copy-start.8 = (bf16[2,256,128]{2,1,0:T(8,128)(2,1)S(1)}, bf16[2,256,128]{2,1,0:T(8,128)(2,1)}, u32[]{:S(2)}) copy-start(bf16[2,256,128]{2,1,0:T(8,128)(2,1)} %constant.23.clone.halo_ref) | copy-start | bytes 393220
  6.0 0.8 %copy-start.9 = (bf16[2,128,128]{2,1,0:T(8,128)(2,1)S(1)}, bf16[2,128,128]{2,1,0:T(8,128)(2,1)}, u32[]{:S(2)}) copy-start(bf16[2,128,128]{2,1,0:T(8,128)(2,1)} %constant.18.clone.first_ref) | copy-start | bytes 196612
  6.9 0.8 %copy-start.10 = (f32[2,64,128]{2,1,0:T(8,128)S(1)}, f32[2,64,128]{2,1,0:T(8,128)}, u32[]{:S(2)}) copy-start(f32[2,64,128]{2,1,0:T(8,128)} %constant.19.clone.twiddle_ref) | copy-start | bytes 196612
  11.4 1.0 %copy-start = (f32[32,72,128]{2,1,0:T(8,128)}, f32[32,72,128]{2,1,0:T(8,128)S(1)}, u32[]{:S(2)}) copy-start(f32[32,72,128]{2,1,0:T(8,128)S(1)} %range_compress.1.send_ref) | copy-start | bytes 3538948
  12.4 33.2 %copy-start.13 = (f32[256]{0:T(256)S(1)}, f32[256]{0:T(256)}, u32[]{:S(2)}) copy-start(f32[256]{0:T(256)} %param.20) | copy-start | bytes 3076
  12.4 33.3 %copy-start.14 = (s32[256]{0:T(256)S(1)}, s32[256]{0:T(256)}, u32[]{:S(2)}) copy-start(s32[256]{0:T(256)} %param.21) | copy-start | bytes 3076
  12.4 33.5 %copy-start.15 = (s32[256]{0:T(256)S(1)}, s32[256]{0:T(256)}, u32[]{:S(2)}) copy-start(s32[256]{0:T(256)} %param.22) | copy-start | bytes 3076
  12.4 33.6 %copy-start.6 = (bf16[2,256,256]{2,1,0:T(8,128)(2,1)S(1)}, bf16[2,256,256]{2,1,0:T(8,128)(2,1)}, u32[]{:S(2)}) copy-start(bf16[2,256,256]{2,1,0:T(8,128)(2,1)} %constant.24.clone.doppler_ref) | copy-start | bytes 786436
  12.4 33.6 %copy-start.7 = (bf16[2,2,128,256]{3,2,1,0:T(8,128)(2,1)S(1)}, bf16[2,2,128,256]{3,2,1,0:T(8,128)(2,1)}, u32[]{:S(2)}) copy-start(bf16[2,2,128,256]{3,2,1,0:T(8,128)(2,1)} %constant.25.clone.halo_doppler_ref) | copy-start | bytes 786436
  12.4 33.6 %copy-start.11 = (f32[2,4,4,128]{3,2,1,0:T(4,128)S(1)}, f32[2,4,4,128]{3,2,1,0:T(4,128)}, u32[]{:S(2)}) copy-start(f32[2,4,4,128]{3,2,1,0:T(4,128)} %param.18) | copy-start | bytes 49156
  12.4 33.6 %copy-start.12 = (s32[4]{0:T(128)S(1)}, s32[4]{0:T(128)}, u32[]{:S(2)}) copy-start(s32[4]{0:T(128)} %delays_ref.1) | copy-start | bytes 52
  46.1 1.3 %copy-start.1 = (f32[32,72,128]{2,1,0:T(8,128)S(1)}, f32[32,72,128]{2,1,0:T(8,128)}, u32[]{:S(2)}) copy-start(f32[32,72,128]{2,1,0:T(8,128)} %exchange.1) | copy-start | bytes 3538948

commit v2 on v1

--- a/solution.py
+++ b/solution.py
@@ -13,6 +13,7 @@
 MIG = 16
 LANES = 128
 HALO_ROWS = 8
+KERNEL_VMEM = 62 * 1024 * 1024
 
 
 highest = lax.Precision.HIGHEST
@@ -243,21 +244,150 @@
     )
 
 
-def range_kernel(
-    sizes, x_ref, chirp_ref, first_ref, twiddle_ref, fwd_ref, inv_ref, last_ref, halo_ref, out_ref
+def spread_rows(values):
+    return jnp.concatenate(
+        [
+            jnp.broadcast_to(values[h : h + 1, :], (LANES, LANES)).T
+            for h in range(values.shape[0])
+        ],
+        axis=0,
+    )
+
+
+def compress_kernel(
+    sizes,
+    x_hbm,
+    chirp_hbm,
+    rate_hbm,
+    band_hbm,
+    migration_hbm,
+    first_hbm,
+    twiddle_hbm,
+    fwd_hbm,
+    inv_hbm,
+    last_hbm,
+    halo_hbm,
+    recv_ref,
+    cos_hbm,
+    sin_hbm,
+    reach_hbm,
+    square_hbm,
+    x_ref,
+    chirp_ref,
+    rate_ref,
+    band_ref,
+    migration_ref,
+    first_ref,
+    twiddle_ref,
+    fwd_ref,
+    inv_ref,
+    last_ref,
+    halo_ref,
+    send_ref,
+    rows_ref,
+    cos_ref,
+    sin_ref,
+    reach_ref,
+    square_ref,
+    load_sems,
+    store_sems,
+    local_sem,
+    send_sems,
+    recv_sems,
 ):
-    pulses, channels, lead, devices = sizes
-    tw_r = jnp.concatenate([twiddle_ref[0]] * channels, axis=0)
-    tw_i = jnp.concatenate([twiddle_ref[1]] * channels, axis=0)
-    chirp_r = jnp.concatenate([chirp_ref[0]] * channels, axis=0)
-    chirp_i = jnp.concatenate([chirp_ref[1]] * channels, axis=0)
+    pulses, channels, lead, devices, inner, length = sizes
+    mine = lax.axis_index("az") * inner + lax.axis_index("rg")
+    barrier = pltpu.get_barrier_semaphore()
+
+    def place(index):
+        return (lax.div(index, inner), lax.rem(index, inner))
+
+    def greet(k, carry):
+        pl.semaphore_signal(
+            barrier,
+            inc=1,
+            device_id=place(lax.rem(mine + k, devices)),
+            device_id_type=pl.DeviceIdType.MESH,
+        )
+        return carry
+
+    loads = []
+
+    def start_load(source, target):
+        copy = pltpu.make_async_copy(source, target, load_sems.at[len(loads)])
+        copy.start()
+        loads.append(copy)
+        return copy
+
+    def pulse_load(p):
+        at = pl.ds(p * channels, channels)
+        return start_load(x_hbm.at[at], x_ref.at[at])
+
+    load_x = [pulse_load(0)]
+    load_first = start_load(first_hbm, first_ref)
+    load_twiddle = start_load(twiddle_hbm, twiddle_ref)
+    load_fwd = start_load(fwd_hbm, fwd_ref)
+    load_chirp = start_load(chirp_hbm, chirp_ref)
+    load_inv = start_load(inv_hbm, inv_ref)
+    load_last = start_load(last_hbm, last_ref)
+    load_x += [pulse_load(p) for p in range(1, pulses)]
+    load_halo = start_load(halo_hbm, halo_ref)
+    load_rate = start_load(rate_hbm, rate_ref)
+    load_band = start_load(band_hbm, band_ref)
+    load_migration = start_load(migration_hbm, migration_ref)
+    lax.fori_loop(1, devices, greet, 0)
+
+    rows = pulses * channels * 4 + HALO_ROWS
+    cut = channels * 4
+
+    def remote(chunk, i):
+        far = lax.div(i + 1, 2)
+        step = devices // 2 + far - 2 * far * lax.rem(i, 2)
+        target = lax.rem(mine + step, devices)
+        at = pl.ds(0, cut) if chunk == 0 else pl.ds(cut, rows - cut)
+        return pltpu.make_async_remote_copy(
+            src_ref=send_ref.at[target, at],
+            dst_ref=recv_ref.at[mine, at],
+            send_sem=send_sems.at[chunk, step],
+            recv_sem=recv_sems.at[chunk, step],
+            device_id=place(target),
+            device_id_type=pl.DeviceIdType.MESH,
+        )
+
+    def send(chunk):
+        def body(i, carry):
+            remote(chunk, i).start()
+            return carry
+
+        lax.fori_loop(0, devices - 1, body, 0)
+
     lane = lax.broadcasted_iota(jnp.int32, (2 * lead, LANES), 1)
     groups = pulses * channels * MIG // LANES
     per_group = LANES // MIG
+    pairs = channels // 2
     packs = [jnp.zeros((2 * lead, LANES), jnp.float32) for _ in range(groups)]
     for p in range(pulses):
+        load_x[p].wait()
+        if p == 0:
+            load_first.wait()
         x = jnp.concatenate([x_ref[p * channels + c] for c in range(channels)], axis=1)
         y = dot_left(first_ref, x)
+        if p == 0:
+            load_twiddle.wait()
+            load_fwd.wait()
+            load_chirp.wait()
+            load_inv.wait()
+            tw_r = jnp.concatenate([twiddle_ref[0]] * channels, axis=0)
+            tw_i = jnp.concatenate([twiddle_ref[1]] * channels, axis=0)
+            chirp = jnp.concatenate(
+                [chirp_ref[pl.ds(part, lead, stride=2), :] for part in range(2)], axis=0
+            ).T
+            top, bottom = chirp[:lead], chirp[lead:]
+            left = lane[:lead] < lead
+            chirp_r = jnp.where(left, top, pltpu.roll(bottom, lead, 1))
+            chirp_i = jnp.where(left, pltpu.roll(top, lead, 1), bottom)
+            chirp_r = jnp.concatenate([chirp_r] * channels, axis=0)
+            chirp_i = jnp.concatenate([chirp_i] * channels, axis=0)
         y = jnp.concatenate([y[:, c * LANES : (c + 1) * LANES] for c in range(channels)], axis=0)
         y = y.reshape(channels, 2, lead, LANES)
         y_r = y[:, 0].reshape(channels * lead, LANES)
@@ -278,90 +408,145 @@
             )
             for c in range(channels)
         ]
-        pairs = channels // 2
         stacked = jnp.concatenate(
             [jnp.concatenate([z[2 * k], z[2 * k + 1]], axis=0) for k in range(pairs)], axis=1
         )
+        if p == 0:
+            load_last.wait()
         w = dot_left(last_ref, stacked)
         for k in range(pairs):
             row = (p * pairs + k) * 8
-            out_ref[:, row : row + 8, :] = w[:, k * LANES : (k + 1) * LANES].reshape(
+            send_ref[:, row : row + 8, :] = w[:, k * LANES : (k + 1) * LANES].reshape(
                 devices, 8, LANES
             )
         for c in range(channels):
             signal = p * channels + c
-            g, place = signal // per_group, signal % per_group
-            moved = z[c] if place == 0 else pltpu.roll(z[c], place * MIG, 1)
-            packs[g] = jnp.where(lane // MIG == place, moved, packs[g])
+            g, where = signal // per_group, signal % per_group
+            moved = z[c] if where == 0 else pltpu.roll(z[c], where * MIG, 1)
+            packs[g] = jnp.where(lane // MIG == where, moved, packs[g])
+        if p == 0:
+            pl.semaphore_wait(barrier, devices - 1)
+            send(0)
+    load_halo.wait()
     w = dot_left(halo_ref, jnp.concatenate(packs, axis=1))
     row = lax.broadcasted_iota(jnp.int32, (devices * HALO_ROWS, LANES), 0) % HALO_ROWS
     total = w[:, :LANES]
     for g in range(1, groups):
         total = jnp.where(row // 2 == g, w[:, g * LANES : (g + 1) * LANES], total)
-    out_ref[:, pulses * channels * 4 :, :] = total.reshape(devices, HALO_ROWS, LANES)
-
-
-def exchange_kernel(devices, inner, send_ref, recv_ref, local_sem, send_sems, recv_sems):
-    mine = lax.axis_index("az") * inner + lax.axis_index("rg")
-    barrier = pltpu.get_barrier_semaphore()
-
-    def place(index):
-        return (lax.div(index, inner), lax.rem(index, inner))
-
-    for k in range(1, devices):
-        pl.semaphore_signal(
-            barrier,
-            inc=1,
-            device_id=place(lax.rem(mine + k, devices)),
-            device_id_type=pl.DeviceIdType.MESH,
-        )
+    send_ref[:, pulses * channels * 4 :, :] = total.reshape(devices, HALO_ROWS, LANES)
+    send(1)
     own = pltpu.make_async_copy(send_ref.at[mine], recv_ref.at[mine], local_sem)
     own.start()
-    pl.semaphore_wait(barrier, devices - 1)
-    copies = []
-    for k in range(devices // 2, 0, -1):
-        for step in sorted({k, devices - k}):
-            target = lax.rem(mine + step, devices)
-            copy = pltpu.make_async_remote_copy(
-                src_ref=send_ref.at[target],
-                dst_ref=recv_ref.at[mine],
-                send_sem=send_sems.at[step],
-                recv_sem=recv_sems.at[step],
-                device_id=place(target),
-                device_id_type=pl.DeviceIdType.MESH,
+
+    load_rate.wait()
+    load_band.wait()
+    load_migration.wait()
+    rows_ref[0] = spread_rows(rate_ref[...])
+    rows_ref[1] = spread_rows(band_ref[...].astype(jnp.float32))
+    rows_ref[2] = spread_rows(migration_ref[...].astype(jnp.float32))
+    bins = rows_ref.shape[1]
+
+    def tables(index, carry):
+        at = pl.ds(pl.multiple_of(index * 8, 8), 8)
+        rate = rows_ref[0, at, :]
+        band = rows_ref[1, at, :].astype(jnp.int32)
+        move = rows_ref[2, at, :].astype(jnp.int32)
+        band_square = band * band
+        square_ref[at, :] = band_square
+        for start in range(0, length, LANES):
+            doppler = lax.broadcasted_iota(jnp.int32, (8, LANES), 1) + start
+            centred = jnp.where(doppler >= length // 2, doppler - length, doppler)
+            relative = centred.astype(jnp.float32) * (2.0 / length)
+            cosine, sine = cos_sin_turns(rate * (relative * relative * (curvature / 2.0)))
+            inside = jnp.abs(centred) < band
+            columns = slice(start, start + LANES)
+            cos_ref[at, columns] = jnp.where(inside, cosine, 0.0)
+            sin_ref[at, columns] = jnp.where(inside, sine, 0.0)
+            reach_ref[at, columns] = move * jnp.minimum(centred * centred, band_square) + (
+                band_square >> 1
             )
-            copy.start()
-            copies.append(copy)
+        return carry
+
+    lax.fori_loop(0, bins // 8, tables, 0)
+    stores = []
+    for source, target in (
+        (cos_ref, cos_hbm),
+        (sin_ref, sin_hbm),
+        (reach_ref, reach_hbm),
+        (square_ref, square_hbm),
+    ):
+        copy = pltpu.make_async_copy(source, target, store_sems.at[len(stores)])
+        copy.start()
+        stores.append(copy)
+    for copy in stores:
+        copy.wait()
     own.wait()
-    for copy in copies:
-        copy.wait()
+
+    def finish(i, carry):
+        for chunk in range(2):
+            copy = remote(chunk, i)
+            copy.wait_send()
+            copy.wait_recv()
+        return carry
+
+    lax.fori_loop(0, devices - 1, finish, 0)
 
 
 def azimuth_kernel(
     sizes,
-    recv_ref,
+    recv_hbm,
     reconstruction_ref,
     delays_ref,
-    rate_ref,
-    band_ref,
-    migration_ref,
     doppler_ref,
     halo_doppler_ref,
     final_hbm,
+    cos_hbm,
+    sin_hbm,
+    reach_hbm,
+    square_hbm,
     out_ref,
+    recv_ref,
     spectra,
     unfolded,
     focused,
     mix,
     final,
-    final_sem,
+    cos_ref,
+    sin_ref,
+    reach_ref,
+    square_ref,
+    load_sems,
+    recv_sems,
 ):
     sources, local_pulses, channels, bins = sizes
     pulses = sources * local_pulses
     block = local_pulses * channels * 4 + HALO_ROWS
     length = channels * pulses
-    load = pltpu.make_async_copy(final_hbm, final, final_sem)
-    load.start()
+    arrivals = []
+
+    def arrive(row):
+        at = pl.ds(row, 8)
+        copy = pltpu.make_async_copy(
+            recv_hbm.at[:, at], recv_ref.at[:, at], recv_sems.at[len(arrivals)]
+        )
+        copy.start()
+        arrivals.append(copy)
+
+    for pair in range(channels // 2):
+        for p in range(local_pulses):
+            arrive((p * (channels // 2) + pair) * 8)
+    arrive(local_pulses * channels * 4)
+    loads = []
+    for source, target in (
+        (reach_hbm, reach_ref),
+        (square_hbm, square_ref),
+        (cos_hbm, cos_ref),
+        (sin_hbm, sin_ref),
+        (final_hbm, final),
+    ):
+        copy = pltpu.make_async_copy(source, target, load_sems.at[len(loads)])
+        copy.start()
+        loads.append(copy)
 
     row = lax.broadcasted_iota(jnp.int32, (channels * channels, pulses), 0) % channels
     frequency = lax.broadcasted_iota(jnp.int32, (channels * channels, pulses), 1)
@@ -375,9 +560,13 @@
     mix[1] = rec_r * align_i + rec_i * align_r
 
     def rows_of(start):
-        return recv_ref[pl.ds(start, sources, stride=block), :]
-
+        return flat[pl.ds(start, sources, stride=block), :]
+
+    flat = recv_ref.reshape(sources * block, LANES)
     for c in range(channels):
+        if c % 2 == 0:
+            for p in range(local_pulses):
+                arrivals[c // 2 * local_pulses + p].wait()
         for half in range(bins // LANES):
             z = jnp.concatenate(
                 [
@@ -390,6 +579,7 @@
             spectra[c, half * LANES : (half + 1) * LANES, :] = dot_right(z.T, doppler_ref)
     groups = local_pulses * channels * MIG // LANES
     per_group = LANES // (MIG * channels)
+    arrivals[-1].wait()
     h = jnp.concatenate(
         [
             rows_of(local_pulses * channels * 4 + g * 2 + part)
@@ -425,23 +615,17 @@
 
     lax.fori_loop(0, (bins + MIG) // 8, mix_rows, 0)
 
+    for copy in loads[:-1]:
+        copy.wait()
+
     def focus_band(b, carry):
         lane = pl.multiple_of(b * LANES, LANES)
         at_real = pl.ds(lane, LANES)
         at_imag = pl.ds(pl.multiple_of(length + lane, LANES), LANES)
-        doppler = lax.broadcasted_iota(jnp.int32, (8, LANES), 1) + lane
-        centred = doppler - jnp.where(doppler >= length // 2, length, 0)
-        centred_square = centred * centred
-        distance = jnp.abs(centred)
-        relative = centred.astype(jnp.float32) * (2.0 / length)
-        chirp_turns = relative * relative * (curvature / 2.0)
         for start in range(0, bins, 8):
             at = slice(start, start + 8)
-            rate = jnp.broadcast_to(rate_ref[at, :], (8, LANES))
-            band = jnp.broadcast_to(band_ref[at, :], (8, LANES))
-            move = jnp.broadcast_to(migration_ref[at, :], (8, LANES))
-            band_square = band * band
-            reach = move * jnp.minimum(centred_square, band_square) + (band_square >> 1)
+            band_square = square_ref[at, :]
+            reach = reach_ref[at, at_real]
             real = unfolded[at, at_real]
             imag = unfolded[at, at_imag]
             bound = band_square
@@ -451,14 +635,14 @@
                 real = jnp.where(moved, unfolded[window, at_real], real)
                 imag = jnp.where(moved, unfolded[window, at_imag], imag)
                 bound = bound + band_square
-            cosine, sine = cos_sin_turns(rate * chirp_turns)
-            inside = distance < band
-            focused[at, at_real] = jnp.where(inside, real * cosine - imag * sine, 0.0)
-            focused[at, at_imag] = jnp.where(inside, real * sine + imag * cosine, 0.0)
+            cosine = cos_ref[at, at_real]
+            sine = sin_ref[at, at_real]
+            focused[at, at_real] = real * cosine - imag * sine
+            focused[at, at_imag] = real * sine + imag * cosine
         return carry
 
     lax.fori_loop(0, length // LANES, focus_band, 0)
-    load.wait()
+    loads[-1].wait()
     image = dot_right(focused[...], final)
     out_ref[0] = image[:, :length]
     out_ref[1] = image[:, length:]
@@ -474,13 +658,17 @@
         and length % (LANES * devices) == 0
         and bins == 2 * LANES
         and channels % 2 == 0
-        and lead % 8 == 0
+        and 2 * lead == LANES
         and devices % 8 == 0
         and signals * MIG % LANES == 0
         and LANES % (MIG * channels) == 0
         and 2 * (signals * MIG // LANES) <= HALO_ROWS
         and channels * pulses <= 512
     )
+
+
+def hbm():
+    return pl.BlockSpec(memory_space=pltpu.HBM)
 
 
 def vmem():
@@ -503,8 +691,9 @@
 
     first = left_matrix(*roots(leads, leads, lead, -1.0))
     first = first.transpose(0, 1, 3, 2).reshape(2 * lead, 2 * lead)
-    forward = right_matrix(*roots(lanes, lanes, LANES, -1.0)).reshape(2 * LANES, 2 * LANES)
-    inverse = right_matrix(*roots(lanes, lanes, LANES, 1.0)).reshape(2 * LANES, 2 * LANES)
+    turned = np.concatenate([lanes[0::2], lanes[1::2]])
+    forward = right_matrix(*roots(lanes, turned, LANES, -1.0)).reshape(2 * LANES, 2 * LANES)
+    inverse = right_matrix(*roots(turned, lanes, LANES, 1.0)).reshape(2 * LANES, 2 * LANES)
     last = left_matrix(*roots(leads, leads, lead, 1.0)) / length
     pair = np.zeros((devices, 2, 2, 2, 2, 2 * lead))
     by_device = last.reshape(2, devices, 2, 2 * lead).transpose(1, 0, 2, 3)
@@ -543,18 +732,16 @@
 
     x = raw_echoes.reshape(signals, 2, lead, LANES).transpose(0, 2, 1, 3)
     x = x.reshape(signals, 2 * lead, LANES)
-    chirp = chirp_spectrum.reshape(2, LANES, lead).transpose(0, 2, 1)
+    chirp = chirp_spectrum.reshape(2, lead, LANES).transpose(1, 0, 2).reshape(2 * lead, LANES)
     block = signals * 4 + HALO_ROWS
-    send = pl.pallas_call(
-        functools.partial(range_kernel, (local_pulses, channels, lead, devices)),
-        out_shape=jax.ShapeDtypeStruct((devices, block, LANES), jnp.float32),
-        in_specs=[vmem()] * 8,
-        out_specs=vmem(),
-        compiler_params=pltpu.CompilerParams(vmem_limit_bytes=48 * 1024 * 1024),
-        name="range_compress",
-    )(
+    tables = (bins, doppler_bins)
+    by_lane = (bins // LANES, LANES)
+    operands = (
         x,
         chirp,
+        azimuth_rate.reshape(by_lane),
+        band_halfwidth.reshape(by_lane),
+        migration.reshape(by_lane),
         split_constant(first),
         twiddles,
         split_constant(forward),
@@ -562,55 +749,81 @@
         split_constant(pair),
         split_constant(halo),
     )
-    received = pl.pallas_call(
-        functools.partial(exchange_kernel, devices, inner),
-        out_shape=jax.ShapeDtypeStruct((devices, block, LANES), jnp.float32),
-        in_specs=[pl.BlockSpec(memory_space=pl.ANY)],
-        out_specs=pl.BlockSpec(memory_space=pl.ANY),
-        scratch_shapes=[
+    received, cosine, sine, reach, square = pl.pallas_call(
+        functools.partial(
+            compress_kernel, (local_pulses, channels, lead, devices, inner, doppler_bins)
+        ),
+        out_shape=(
+            jax.ShapeDtypeStruct((devices, block, LANES), jnp.float32),
+            jax.ShapeDtypeStruct(tables, jnp.float32),
+            jax.ShapeDtypeStruct(tables, jnp.float32),
+            jax.ShapeDtypeStruct(tables, jnp.int32),
+            jax.ShapeDtypeStruct((bins, LANES), jnp.int32),
+        ),
+        in_specs=[hbm()] * len(operands),
+        out_specs=(hbm(),) * 5,
+        scratch_shapes=[pltpu.VMEM(value.shape, value.dtype) for value in operands]
+        + [
+            pltpu.VMEM((devices, block, LANES), jnp.float32),
+            pltpu.VMEM((3, bins, LANES), jnp.float32),
+            pltpu.VMEM(tables, jnp.float32),
+            pltpu.VMEM(tables, jnp.float32),
+            pltpu.VMEM(tables, jnp.int32),
+            pltpu.VMEM((bins, LANES), jnp.int32),
+            pltpu.SemaphoreType.DMA((len(operands) + local_pulses - 1,)),
+            pltpu.SemaphoreType.DMA((4,)),
             pltpu.SemaphoreType.DMA,
-            pltpu.SemaphoreType.DMA((devices,)),
-            pltpu.SemaphoreType.DMA((devices,)),
+            pltpu.SemaphoreType.DMA((2, devices)),
+            pltpu.SemaphoreType.DMA((2, devices)),
         ],
-        compiler_params=pltpu.CompilerParams(collective_id=0, has_side_effects=True),
-        name="exchange",
-    )(send)
-    received = received.reshape(devices * block, LANES)
+        compiler_params=pltpu.CompilerParams(
+            collective_id=0, has_side_effects=True, vmem_limit_bytes=KERNEL_VMEM
+        ),
+        name="compress_exchange",
+    )(*operands)
     return pl.pallas_call(
         functools.partial(azimuth_kernel, (devices, local_pulses, channels, bins)),
         out_shape=jax.ShapeDtypeStruct((2, bins, doppler_bins), jnp.float32),
         in_specs=[
-            vmem(),
+            hbm(),
             vmem(),
             pl.BlockSpec(memory_space=pltpu.SMEM),
             vmem(),
             vmem(),
-            vmem(),
-            vmem(),
-            vmem(),
-            pl.BlockSpec(memory_space=pl.ANY),
+            hbm(),
+            hbm(),
+            hbm(),
+            hbm(),
+            hbm(),
         ],
         out_specs=vmem(),
         scratch_shapes=[
+            pltpu.VMEM((devices, block, LANES), jnp.float32),
             pltpu.VMEM((channels, bins + MIG, 2 * pulses), jnp.float32),
             pltpu.VMEM((bins + MIG, 2 * doppler_bins), jnp.float32),
             pltpu.VMEM((bins, 2 * doppler_bins), jnp.float32),
             pltpu.VMEM((2, channels * channels, pulses), jnp.float32),
             pltpu.VMEM((2, 2 * doppler_bins, 2 * doppler_bins), jnp.bfloat16),
-            pltpu.SemaphoreType.DMA,
+            pltpu.VMEM(tables, jnp.float32),
+            pltpu.VMEM(tables, jnp.float32),
+            pltpu.VMEM(tables, jnp.int32),
+            pltpu.VMEM((bins, LANES), jnp.int32),
+            pltpu.SemaphoreType.DMA((5,)),
+            pltpu.SemaphoreType.DMA((channels // 2 * local_pulses + 1,)),
         ],
-        compiler_params=pltpu.CompilerParams(vmem_limit_bytes=48 * 1024 * 1024),
+        compiler_params=pltpu.CompilerParams(vmem_limit_bytes=KERNEL_VMEM),
         name="azimuth_focus",
     )(
         received,
         reconstruction.reshape(2, channels * channels, pulses),
         delays,
-        azimuth_rate.reshape(bins, 1),
-        band_halfwidth.reshape(bins, 1),
-        migration.reshape(bins, 1),
         split_constant(to_doppler),
         halo_doppler,
         split_constant(final),
+        cosine,
+        sine,
+        reach,
+        square,
     )
 
 

time: 55.7 us -> 43.1 us (0.77)
  local copies, waits for them, and re-layouts: 10.4 us -> 0 us
  Pallas kernels: 44.7 us -> 42.9 us
    unnamed x32 -> x0, local copies, waits for them, and re-layouts: 8.98 us -> none
    pallas_call x2 -> x1, Pallas kernels: 36.7 us -> 33.8 us  [blocked_local(): pl.pallas_call(functools.partial(compress_kernel, (local_pulses, channels...]
    reshape x5 -> x0, local copies, waits for them, and re-layouts: 1.45 us -> none  [the longest x2 1.05 us: blocked_local(): chirp = chirp_spectrum.reshape(2, LANES, lead).transpose(0, 2, 1)]
    pallas_call x1, Pallas kernels: 7.92 us -> 9.12 us  [blocked_local(): pl.pallas_call(functools.partial(azimuth_kernel, (devices, local_pulses,...]
where the time goes in v2:
time: 43.1 us; the launch traced here: 42.9 us
  Pallas kernels  42.9 us (100%)
    pallas_call x1, Pallas kernels, blocked_local(): pl.pallas_call(functools.partial(compress_kernel, (local_pulses, channels...  33.8 us
    pallas_call x1, Pallas kernels, blocked_local(): pl.pallas_call(functools.partial(azimuth_kernel, (devices, local_pulses,...  9.12 us

profile of v2, /device:TPU:0, one launch (start us, length us, event | category | flops | bytes accessed | tf_op | source)
XLA Modules:
  0.0 42.9 jit_solution(14999301866185453598)
XLA Ops:
  0.0 33.8 %compress_exchange.1 = (f32[32,72,128]{2,1,0:T(8,128)}, f32[256,512]{1,0:T(8,128)}, f32[256,512]{1,0:T(8,128)}, s32[256,512]{1,0:T(8,128)}, s32[256,128]{1,0:T(8,128)}) custom-call(f32[16,128,128]{2,1,0:T(8,128)} %bitcast.14, f32[128,128]{1,0:T(8,128)} %bitcast.15, f32[2,128]{1,0:T(2,128)} %bitcast.17, s32[2,128]{1,0:T(2,128)} %bitcast.18, ...), custom_call_target="tpu_custom_call" | custom-call | tf_op jit(solution)/shard_map/compress_exchange/pallas_call | solution.py:752
  33.8 9.1 %azimuth_focus.1 = f32[2,256,512]{2,1,0:T(8,128)} custom-call(f32[32,72,128]{2,1,0:T(8,128)} %get-tuple-element.10.recv_hbm, f32[2,16,128]{2,1,0:T(8,128)} %bitcast.16, s32[4]{0:T(128)} %delays_ref.1, bf16[2,256,256]{2,1,0:T(8,128)(2,1)} %constant.24.clone.doppler_ref, bf16[2,2,128,256]{3,2,1,0:T(8,128)(2,1)} %constant.25.clone.halo_doppler_ref, ...), custom_call_target="tpu_custom_call" | custom-call | tf_op jit(solution)/shard_map/azimuth_focus/pallas_call | solution.py:784

commit v3 on v2

--- a/solution.py
+++ b/solution.py
@@ -254,6 +254,74 @@
     )
 
 
+def doppler_bins_of(flat, sources, block, channel, pulses, matrix):
+    z = jnp.concatenate(
+        [
+            flat[pl.ds(p * 8 + channel * 2 + part, sources, stride=block), :]
+            for part in range(2)
+            for p in range(pulses)
+        ],
+        axis=0,
+    )
+    return dot_right(z.T, matrix)
+
+
+def mix_channels(spectra, mix, unfolded, rows, shift):
+    channels = spectra.shape[0]
+    pulses = spectra.shape[2] // 2
+    length = channels * pulses
+
+    def mix_rows(index, carry):
+        at = pl.ds(pl.multiple_of(index * 8, 8), 8)
+        to = pl.ds(pl.multiple_of(index * 8 + shift, 8), 8)
+        spec = [spectra[c, at, :] for c in range(channels)]
+        for b in range(channels):
+            total_r = total_i = None
+            for c in range(channels):
+                m = b * channels + c
+                m_r = jnp.broadcast_to(mix[0, m : m + 1, :], (8, pulses))
+                m_i = jnp.broadcast_to(mix[1, m : m + 1, :], (8, pulses))
+                d_r, d_i = spec[c][:, :pulses], spec[c][:, pulses:]
+                r = m_r * d_r - m_i * d_i
+                i = m_r * d_i + m_i * d_r
+                total_r = r if c == 0 else total_r + r
+                total_i = i if c == 0 else total_i + i
+            unfolded[to, b * pulses : (b + 1) * pulses] = total_r
+            unfolded[to, length + b * pulses : length + (b + 1) * pulses] = total_i
+        return carry
+
+    lax.fori_loop(0, rows // 8, mix_rows, 0)
+
+
+def focus_rows(unfolded, cos_ref, sin_ref, reach_ref, square_ref, focused, rows):
+    length = reach_ref.shape[1]
+
+    def focus_band(b, carry):
+        lane = pl.multiple_of(b * LANES, LANES)
+        at_real = pl.ds(lane, LANES)
+        at_imag = pl.ds(pl.multiple_of(length + lane, LANES), LANES)
+        for start in range(0, rows, 8):
+            at = slice(start, start + 8)
+            band_square = square_ref[at, :]
+            reach = reach_ref[at, at_real]
+            real = unfolded[at, at_real]
+            imag = unfolded[at, at_imag]
+            bound = band_square
+            for offset in range(1, MIG + 1):
+                moved = reach >= bound
+                window = slice(start + offset, start + offset + 8)
+                real = jnp.where(moved, unfolded[window, at_real], real)
+                imag = jnp.where(moved, unfolded[window, at_imag], imag)
+                bound = bound + band_square
+            cosine = cos_ref[at, at_real]
+            sine = sin_ref[at, at_real]
+            focused[at, at_real] = real * cosine - imag * sine
+            focused[at, at_imag] = real * sine + imag * cosine
+        return carry
+
+    lax.fori_loop(0, length // LANES, focus_band, 0)
+
+
 def compress_kernel(
     sizes,
     x_hbm,
@@ -267,11 +335,19 @@
     inv_hbm,
     last_hbm,
     halo_hbm,
-    recv_ref,
+    reconstruction_hbm,
+    delays_hbm,
+    doppler_hbm,
+    final_hbm,
+    late_ref,
+    late_halo_ref,
     cos_hbm,
     sin_hbm,
     reach_hbm,
     square_hbm,
+    mix_hbm,
+    edge_hbm,
+    image_hbm,
     x_ref,
     chirp_ref,
     rate_ref,
@@ -283,15 +359,26 @@
     inv_ref,
     last_ref,
     halo_ref,
+    reconstruction_ref,
+    delays_ref,
+    doppler_ref,
+    final_ref,
     send_ref,
+    send_halo_ref,
+    early_ref,
     rows_ref,
     cos_ref,
     sin_ref,
     reach_ref,
     square_ref,
+    mix_ref,
+    spectra,
+    unfolded,
+    focused,
+    image_ref,
     load_sems,
     store_sems,
-    local_sem,
+    local_sems,
     send_sems,
     recv_sems,
 ):
@@ -335,19 +422,33 @@
     load_rate = start_load(rate_hbm, rate_ref)
     load_band = start_load(band_hbm, band_ref)
     load_migration = start_load(migration_hbm, migration_ref)
+    load_reconstruction = start_load(reconstruction_hbm, reconstruction_ref)
+    load_delays = start_load(delays_hbm, delays_ref)
+    load_doppler = start_load(doppler_hbm, doppler_ref)
+    load_final = start_load(final_hbm, final_ref)
     lax.fori_loop(1, devices, greet, 0)
 
-    rows = pulses * channels * 4 + HALO_ROWS
-    cut = channels * 4
+    half_rows = pulses * 8
+
+    def parts(chunk, target):
+        if chunk == 0:
+            at = pl.ds(0, 8)
+            return send_ref.at[target, at], early_ref.at[mine, at]
+        if chunk == 1:
+            at = pl.ds(8, half_rows - 8)
+            return send_ref.at[target, at], early_ref.at[mine, at]
+        if chunk == 2:
+            return send_ref.at[target, pl.ds(half_rows, half_rows)], late_ref.at[mine]
+        return send_halo_ref.at[target], late_halo_ref.at[mine]
 
     def remote(chunk, i):
         far = lax.div(i + 1, 2)
         step = devices // 2 + far - 2 * far * lax.rem(i, 2)
         target = lax.rem(mine + step, devices)
-        at = pl.ds(0, cut) if chunk == 0 else pl.ds(cut, rows - cut)
+        source, landing = parts(chunk, target)
         return pltpu.make_async_remote_copy(
-            src_ref=send_ref.at[target, at],
-            dst_ref=recv_ref.at[mine, at],
+            src_ref=source,
+            dst_ref=landing,
             send_sem=send_sems.at[chunk, step],
             recv_sem=recv_sems.at[chunk, step],
             device_id=place(target),
@@ -414,11 +515,10 @@
         if p == 0:
             load_last.wait()
         w = dot_left(last_ref, stacked)
-        for k in range(pairs):
-            row = (p * pairs + k) * 8
-            send_ref[:, row : row + 8, :] = w[:, k * LANES : (k + 1) * LANES].reshape(
-                devices, 8, LANES
-            )
+        line = lax.broadcasted_iota(jnp.int32, (w.shape[0], LANES), 0) % 8
+        whole = jnp.where(line < 4, w[:, :LANES], w[:, LANES:]).reshape(2, devices, 8, LANES)
+        send_ref[:, p * 8 : p * 8 + 8, :] = whole[0]
+        send_ref[:, half_rows + p * 8 : half_rows + p * 8 + 8, :] = whole[1]
         for c in range(channels):
             signal = p * channels + c
             g, where = signal // per_group, signal % per_group
@@ -427,17 +527,42 @@
         if p == 0:
             pl.semaphore_wait(barrier, devices - 1)
             send(0)
+    send(1)
+    send(2)
     load_halo.wait()
     w = dot_left(halo_ref, jnp.concatenate(packs, axis=1))
     row = lax.broadcasted_iota(jnp.int32, (devices * HALO_ROWS, LANES), 0) % HALO_ROWS
     total = w[:, :LANES]
     for g in range(1, groups):
         total = jnp.where(row // 2 == g, w[:, g * LANES : (g + 1) * LANES], total)
-    send_ref[:, pulses * channels * 4 :, :] = total.reshape(devices, HALO_ROWS, LANES)
-    send(1)
-    own = pltpu.make_async_copy(send_ref.at[mine], recv_ref.at[mine], local_sem)
-    own.start()
-
+    send_halo_ref[...] = total.reshape(devices, HALO_ROWS, LANES)[:, : 2 * groups, :]
+    send(3)
+    own = [
+        pltpu.make_async_copy(
+            send_ref.at[mine, pl.ds(0, half_rows)], early_ref.at[mine], local_sems.at[0]
+        ),
+        pltpu.make_async_copy(
+            send_ref.at[mine, pl.ds(half_rows, half_rows)], late_ref.at[mine], local_sems.at[1]
+        ),
+        pltpu.make_async_copy(send_halo_ref.at[mine], late_halo_ref.at[mine], local_sems.at[2]),
+    ]
+    for copy in own:
+        copy.start()
+
+    load_reconstruction.wait()
+    load_delays.wait()
+    bins_f = pulses * devices
+    row = lax.broadcasted_iota(jnp.int32, (channels * channels, bins_f), 0) % channels
+    frequency = lax.broadcasted_iota(jnp.int32, (channels * channels, bins_f), 1)
+    delay = jnp.zeros_like(row)
+    for c in range(channels):
+        one = jnp.broadcast_to(delays_ref[0:1, c : c + 1], row.shape)
+        delay = jnp.where(row == c, one, delay)
+    turns = lax.rem(frequency * delay, bins_f).astype(jnp.float32) * (1.0 / bins_f)
+    align_r, align_i = cos_sin_turns(turns)
+    rec_r, rec_i = reconstruction_ref[0], reconstruction_ref[1]
+    mix_ref[0] = rec_r * align_r - rec_i * align_i
+    mix_ref[1] = rec_r * align_i + rec_i * align_r
     load_rate.wait()
     load_band.wait()
     load_migration.wait()
@@ -469,123 +594,129 @@
 
     lax.fori_loop(0, bins // 8, tables, 0)
     stores = []
-    for source, target in (
-        (cos_ref, cos_hbm),
-        (sin_ref, sin_hbm),
-        (reach_ref, reach_hbm),
-        (square_ref, square_hbm),
-    ):
+
+    def store(source, target):
         copy = pltpu.make_async_copy(source, target, store_sems.at[len(stores)])
         copy.start()
         stores.append(copy)
+
+    ready = focused.shape[0]
+    later = pl.ds(ready, bins - ready)
+    store(cos_ref.at[later], cos_hbm)
+    store(sin_ref.at[later], sin_hbm)
+    store(reach_ref.at[later], reach_hbm)
+    store(square_ref.at[later], square_hbm)
+    store(mix_ref, mix_hbm)
+
+    def arrived(chunks):
+        def body(i, carry):
+            for chunk in chunks:
+                remote(chunk, i).wait_recv()
+            return carry
+
+        lax.fori_loop(0, devices - 1, body, 0)
+
+    load_doppler.wait()
+    own[0].wait()
+    arrived((0, 1))
+    flat = early_ref.reshape(devices * half_rows, LANES)
+    for c in range(channels):
+        spectra[c] = doppler_bins_of(flat, devices, half_rows, c, pulses, doppler_ref)
+    mix_channels(spectra, mix_ref, unfolded, ready + MIG, 0)
+    store(unfolded.at[pl.ds(ready, MIG)], edge_hbm)
+    focus_rows(unfolded, cos_ref, sin_ref, reach_ref, square_ref, focused, ready)
+    load_final.wait()
+    image = dot_right(focused[...], final_ref)
+    image_ref[0] = image[:, :length]
+    image_ref[1] = image[:, length:]
+    store(image_ref, image_hbm)
+    for copy in own[1:]:
+        copy.wait()
+    arrived((2, 3))
+
+    def sent(i, carry):
+        for chunk in range(4):
+            remote(chunk, i).wait_send()
+        return carry
+
+    lax.fori_loop(0, devices - 1, sent, 0)
     for copy in stores:
         copy.wait()
-    own.wait()
-
-    def finish(i, carry):
-        for chunk in range(2):
-            copy = remote(chunk, i)
-            copy.wait_send()
-            copy.wait_recv()
-        return carry
-
-    lax.fori_loop(0, devices - 1, finish, 0)
 
 
 def azimuth_kernel(
     sizes,
-    recv_hbm,
-    reconstruction_ref,
-    delays_ref,
-    doppler_ref,
-    halo_doppler_ref,
-    final_hbm,
+    late_hbm,
+    late_halo_hbm,
     cos_hbm,
     sin_hbm,
     reach_hbm,
     square_hbm,
-    out_ref,
-    recv_ref,
-    spectra,
-    unfolded,
-    focused,
-    mix,
-    final,
+    mix_hbm,
+    edge_hbm,
+    image_hbm,
+    doppler_hbm,
+    halo_doppler_hbm,
+    final_hbm,
+    out_hbm,
+    late_ref,
+    late_halo_ref,
     cos_ref,
     sin_ref,
     reach_ref,
     square_ref,
+    mix_ref,
+    doppler_ref,
+    halo_doppler_ref,
+    final_ref,
+    spectra,
+    unfolded,
+    focused,
+    image_ref,
     load_sems,
-    recv_sems,
+    store_sems,
 ):
-    sources, local_pulses, channels, bins = sizes
-    pulses = sources * local_pulses
-    block = local_pulses * channels * 4 + HALO_ROWS
-    length = channels * pulses
-    arrivals = []
-
-    def arrive(row):
-        at = pl.ds(row, 8)
-        copy = pltpu.make_async_copy(
-            recv_hbm.at[:, at], recv_ref.at[:, at], recv_sems.at[len(arrivals)]
-        )
-        copy.start()
-        arrivals.append(copy)
-
-    for pair in range(channels // 2):
-        for p in range(local_pulses):
-            arrive((p * (channels // 2) + pair) * 8)
-    arrive(local_pulses * channels * 4)
+    sources, pulses, channels, bins = sizes
+    length = reach_ref.shape[1]
+    ready = image_hbm.shape[1]
+    rows = bins - ready
     loads = []
-    for source, target in (
-        (reach_hbm, reach_ref),
-        (square_hbm, square_ref),
-        (cos_hbm, cos_ref),
-        (sin_hbm, sin_ref),
-        (final_hbm, final),
-    ):
+
+    def load(source, target):
         copy = pltpu.make_async_copy(source, target, load_sems.at[len(loads)])
         copy.start()
         loads.append(copy)
-
-    row = lax.broadcasted_iota(jnp.int32, (channels * channels, pulses), 0) % channels
-    frequency = lax.broadcasted_iota(jnp.int32, (channels * channels, pulses), 1)
-    delay = jnp.zeros_like(row)
+        return copy
+
+    load_late = load(late_hbm, late_ref)
+    load_doppler = load(doppler_hbm, doppler_ref)
+    load_halo = load(late_halo_hbm, late_halo_ref)
+    load_halo_doppler = load(halo_doppler_hbm, halo_doppler_ref)
+    load_mix = load(mix_hbm, mix_ref)
+    load_tables = [
+        load(edge_hbm, unfolded.at[pl.ds(0, MIG)]),
+        load(reach_hbm, reach_ref),
+        load(square_hbm, square_ref),
+        load(cos_hbm, cos_ref),
+        load(sin_hbm, sin_ref),
+    ]
+    load_final = load(final_hbm, final_ref)
+    passed = load(image_hbm, out_hbm.at[:, pl.ds(0, ready)])
+
+    load_doppler.wait()
+    load_late.wait()
+    half = LANES
+    flat = late_ref.reshape(sources * pulses * 8, LANES)
     for c in range(channels):
-        delay = jnp.where(row == c, delays_ref[c], delay)
-    turns = lax.rem(frequency * delay, pulses).astype(jnp.float32) * (1.0 / pulses)
-    align_r, align_i = cos_sin_turns(turns)
-    rec_r, rec_i = reconstruction_ref[0], reconstruction_ref[1]
-    mix[0] = rec_r * align_r - rec_i * align_i
-    mix[1] = rec_r * align_i + rec_i * align_r
-
-    def rows_of(start):
-        return flat[pl.ds(start, sources, stride=block), :]
-
-    flat = recv_ref.reshape(sources * block, LANES)
-    for c in range(channels):
-        if c % 2 == 0:
-            for p in range(local_pulses):
-                arrivals[c // 2 * local_pulses + p].wait()
-        for half in range(bins // LANES):
-            z = jnp.concatenate(
-                [
-                    rows_of(p * channels * 4 + c * 4 + part * 2 + half)
-                    for part in range(2)
-                    for p in range(local_pulses)
-                ],
-                axis=0,
-            )
-            spectra[c, half * LANES : (half + 1) * LANES, :] = dot_right(z.T, doppler_ref)
-    groups = local_pulses * channels * MIG // LANES
+        spectra[c, :half, :] = doppler_bins_of(
+            flat, sources, pulses * 8, c, pulses, doppler_ref
+        )
+    groups = pulses * channels * MIG // LANES
     per_group = LANES // (MIG * channels)
-    arrivals[-1].wait()
+    load_halo.wait()
+    load_halo_doppler.wait()
     h = jnp.concatenate(
-        [
-            rows_of(local_pulses * channels * 4 + g * 2 + part)
-            for g in range(groups)
-            for part in range(2)
-        ],
+        [late_halo_ref[pl.ds(j, sources, stride=2 * groups), :] for j in range(2 * groups)],
         axis=0,
     ).T
     step = channels * MIG
@@ -593,59 +724,34 @@
     for k in range(1, per_group):
         halo = halo + dot_right(h[k * step : (k + 1) * step], halo_doppler_ref.at[k])
     for c in range(channels):
-        spectra[c, bins:, :] = halo[c * MIG : (c + 1) * MIG]
-
-    def mix_rows(index, carry):
-        at = pl.ds(pl.multiple_of(index * 8, 8), 8)
-        spec = [spectra[c, at, :] for c in range(channels)]
-        for b in range(channels):
-            total_r = total_i = None
-            for c in range(channels):
-                m = b * channels + c
-                m_r = jnp.broadcast_to(mix[0, m : m + 1, :], (8, pulses))
-                m_i = jnp.broadcast_to(mix[1, m : m + 1, :], (8, pulses))
-                d_r, d_i = spec[c][:, :pulses], spec[c][:, pulses:]
-                r = m_r * d_r - m_i * d_i
-                i = m_r * d_i + m_i * d_r
-                total_r = r if c == 0 else total_r + r
-                total_i = i if c == 0 else total_i + i
-            unfolded[at, b * pulses : (b + 1) * pulses] = total_r
-            unfolded[at, length + b * pulses : length + (b + 1) * pulses] = total_i
-        return carry
-
-    lax.fori_loop(0, (bins + MIG) // 8, mix_rows, 0)
-
-    for copy in loads[:-1]:
+        spectra[c, half:, :] = halo[c * MIG : (c + 1) * MIG]
+    load_mix.wait()
+    mix_channels(spectra, mix_ref, unfolded, half + MIG, MIG)
+    for copy in load_tables:
         copy.wait()
-
-    def focus_band(b, carry):
-        lane = pl.multiple_of(b * LANES, LANES)
-        at_real = pl.ds(lane, LANES)
-        at_imag = pl.ds(pl.multiple_of(length + lane, LANES), LANES)
-        for start in range(0, bins, 8):
-            at = slice(start, start + 8)
-            band_square = square_ref[at, :]
-            reach = reach_ref[at, at_real]
-            real = unfolded[at, at_real]
-            imag = unfolded[at, at_imag]
-            bound = band_square
-            for offset in range(1, MIG + 1):
-                moved = reach >= bound
-                window = slice(start + offset, start + offset + 8)
-                real = jnp.where(moved, unfolded[window, at_real], real)
-                imag = jnp.where(moved, unfolded[window, at_imag], imag)
-                bound = bound + band_square
-            cosine = cos_ref[at, at_real]
-            sine = sin_ref[at, at_real]
-            focused[at, at_real] = real * cosine - imag * sine
-            focused[at, at_imag] = real * sine + imag * cosine
-        return carry
-
-    lax.fori_loop(0, length // LANES, focus_band, 0)
-    loads[-1].wait()
-    image = dot_right(focused[...], final)
-    out_ref[0] = image[:, :length]
-    out_ref[1] = image[:, length:]
+    focus_rows(unfolded, cos_ref, sin_ref, reach_ref, square_ref, focused, rows)
+    load_final.wait()
+    high, low = split(focused[...])
+    stores = []
+    pieces = 4
+    width = 2 * length // pieces
+    for k in range(pieces):
+        at = slice(k * width, (k + 1) * width)
+        part = dot(high, final_ref[0, :, at]) + (
+            dot(low, final_ref[0, :, at]) + dot(high, final_ref[1, :, at])
+        )
+        image_ref[k] = part
+        place = (k * width) // length
+        copy = pltpu.make_async_copy(
+            image_ref.at[k],
+            out_hbm.at[place, pl.ds(ready, rows), pl.ds(k * width - place * length, width)],
+            store_sems.at[k],
+        )
+        copy.start()
+        stores.append(copy)
+    passed.wait()
+    for copy in stores:
+        copy.wait()
 
 
 def fits(pulses, channels, length, devices):
@@ -657,7 +763,7 @@
         pulses == LANES
         and length % (LANES * devices) == 0
         and bins == 2 * LANES
-        and channels % 2 == 0
+        and channels == 4
         and 2 * lead == LANES
         and devices % 8 == 0
         and signals * MIG % LANES == 0
@@ -695,11 +801,11 @@
     forward = right_matrix(*roots(lanes, turned, LANES, -1.0)).reshape(2 * LANES, 2 * LANES)
     inverse = right_matrix(*roots(turned, lanes, LANES, 1.0)).reshape(2 * LANES, 2 * LANES)
     last = left_matrix(*roots(leads, leads, lead, 1.0)) / length
-    pair = np.zeros((devices, 2, 2, 2, 2, 2 * lead))
     by_device = last.reshape(2, devices, 2, 2 * lead).transpose(1, 0, 2, 3)
+    pair = np.zeros((2, devices, 2, 2, 2, 2, 2 * lead))
     for s in range(2):
-        pair[:, s, :, :, s, :] = by_device
-    pair = pair.reshape(devices * 8, 4 * lead)
+        pair[:, :, :, s, :, s, :] = by_device.transpose(2, 0, 1, 3)[:, :, None]
+    pair = pair.reshape(devices * 16, 4 * lead)
     halo = np.zeros((devices, HALO_ROWS, 2 * lead))
     groups = signals * MIG // LANES
     for g in range(groups):
@@ -733,9 +839,14 @@
     x = raw_echoes.reshape(signals, 2, lead, LANES).transpose(0, 2, 1, 3)
     x = x.reshape(signals, 2 * lead, LANES)
     chirp = chirp_spectrum.reshape(2, lead, LANES).transpose(1, 0, 2).reshape(2 * lead, LANES)
-    block = signals * 4 + HALO_ROWS
-    tables = (bins, doppler_bins)
     by_lane = (bins // LANES, LANES)
+    halo_rows = 2 * groups
+    half_rows = local_pulses * 8
+    ready = LANES - MIG
+    rest = bins - ready
+    f32, i32, bf16 = jnp.float32, jnp.int32, jnp.bfloat16
+    doppler_matrix = split_constant(to_doppler)
+    final_matrix = split_constant(final)
     operands = (
         x,
         chirp,
@@ -748,83 +859,76 @@
         split_constant(inverse),
         split_constant(pair),
         split_constant(halo),
-    )
-    received, cosine, sine, reach, square = pl.pallas_call(
+        reconstruction.reshape(2, channels * channels, pulses),
+        delays.reshape(1, channels),
+        doppler_matrix,
+        final_matrix,
+    )
+    shapes = (
+        ((devices, half_rows, LANES), f32),
+        ((devices, halo_rows, LANES), f32),
+        ((rest, doppler_bins), f32),
+        ((rest, doppler_bins), f32),
+        ((rest, doppler_bins), i32),
+        ((rest, LANES), i32),
+        ((2, channels * channels, pulses), f32),
+        ((MIG, 2 * doppler_bins), f32),
+        ((2, ready, doppler_bins), f32),
+    )
+    middle = pl.pallas_call(
         functools.partial(
             compress_kernel, (local_pulses, channels, lead, devices, inner, doppler_bins)
         ),
-        out_shape=(
-            jax.ShapeDtypeStruct((devices, block, LANES), jnp.float32),
-            jax.ShapeDtypeStruct(tables, jnp.float32),
-            jax.ShapeDtypeStruct(tables, jnp.float32),
-            jax.ShapeDtypeStruct(tables, jnp.int32),
-            jax.ShapeDtypeStruct((bins, LANES), jnp.int32),
-        ),
+        out_shape=tuple(jax.ShapeDtypeStruct(*shape) for shape in shapes),
         in_specs=[hbm()] * len(operands),
-        out_specs=(hbm(),) * 5,
+        out_specs=(hbm(),) * len(shapes),
         scratch_shapes=[pltpu.VMEM(value.shape, value.dtype) for value in operands]
         + [
-            pltpu.VMEM((devices, block, LANES), jnp.float32),
-            pltpu.VMEM((3, bins, LANES), jnp.float32),
-            pltpu.VMEM(tables, jnp.float32),
-            pltpu.VMEM(tables, jnp.float32),
-            pltpu.VMEM(tables, jnp.int32),
-            pltpu.VMEM((bins, LANES), jnp.int32),
+            pltpu.VMEM((devices, 2 * half_rows, LANES), f32),
+            pltpu.VMEM((devices, halo_rows, LANES), f32),
+            pltpu.VMEM((devices, half_rows, LANES), f32),
+            pltpu.VMEM((3, bins, LANES), f32),
+            pltpu.VMEM((bins, doppler_bins), f32),
+            pltpu.VMEM((bins, doppler_bins), f32),
+            pltpu.VMEM((bins, doppler_bins), i32),
+            pltpu.VMEM((bins, LANES), i32),
+            pltpu.VMEM((2, channels * channels, pulses), f32),
+            pltpu.VMEM((channels, LANES, 2 * pulses), f32),
+            pltpu.VMEM((LANES, 2 * doppler_bins), f32),
+            pltpu.VMEM((ready, 2 * doppler_bins), f32),
+            pltpu.VMEM((2, ready, doppler_bins), f32),
             pltpu.SemaphoreType.DMA((len(operands) + local_pulses - 1,)),
-            pltpu.SemaphoreType.DMA((4,)),
-            pltpu.SemaphoreType.DMA,
-            pltpu.SemaphoreType.DMA((2, devices)),
-            pltpu.SemaphoreType.DMA((2, devices)),
+            pltpu.SemaphoreType.DMA((7,)),
+            pltpu.SemaphoreType.DMA((3,)),
+            pltpu.SemaphoreType.DMA((4, devices)),
+            pltpu.SemaphoreType.DMA((4, devices)),
         ],
         compiler_params=pltpu.CompilerParams(
             collective_id=0, has_side_effects=True, vmem_limit_bytes=KERNEL_VMEM
         ),
         name="compress_exchange",
     )(*operands)
+    late, late_halo = middle[:2]
+    late_halo = late_halo.reshape(devices * halo_rows, LANES)
+    inputs = (late, late_halo, *middle[2:], doppler_matrix, halo_doppler, final_matrix)
+    kept = inputs[:7] + inputs[9:]
     return pl.pallas_call(
         functools.partial(azimuth_kernel, (devices, local_pulses, channels, bins)),
-        out_shape=jax.ShapeDtypeStruct((2, bins, doppler_bins), jnp.float32),
-        in_specs=[
-            hbm(),
-            vmem(),
-            pl.BlockSpec(memory_space=pltpu.SMEM),
-            vmem(),
-            vmem(),
-            hbm(),
-            hbm(),
-            hbm(),
-            hbm(),
-            hbm(),
-        ],
-        out_specs=vmem(),
-        scratch_shapes=[
-            pltpu.VMEM((devices, block, LANES), jnp.float32),
-            pltpu.VMEM((channels, bins + MIG, 2 * pulses), jnp.float32),
-            pltpu.VMEM((bins + MIG, 2 * doppler_bins), jnp.float32),
-            pltpu.VMEM((bins, 2 * doppler_bins), jnp.float32),
-            pltpu.VMEM((2, channels * channels, pulses), jnp.float32),
-            pltpu.VMEM((2, 2 * doppler_bins, 2 * doppler_bins), jnp.bfloat16),
-            pltpu.VMEM(tables, jnp.float32),
-            pltpu.VMEM(tables, jnp.float32),
-            pltpu.VMEM(tables, jnp.int32),
-            pltpu.VMEM((bins, LANES), jnp.int32),
-            pltpu.SemaphoreType.DMA((5,)),
-            pltpu.SemaphoreType.DMA((channels // 2 * local_pulses + 1,)),
+        out_shape=jax.ShapeDtypeStruct((2, bins, doppler_bins), f32),
+        in_specs=[hbm()] * len(inputs),
+        out_specs=hbm(),
+        scratch_shapes=[pltpu.VMEM(value.shape, value.dtype) for value in kept]
+        + [
+            pltpu.VMEM((channels, LANES + MIG, 2 * pulses), f32),
+            pltpu.VMEM((rest + MIG, 2 * doppler_bins), f32),
+            pltpu.VMEM((rest, 2 * doppler_bins), f32),
+            pltpu.VMEM((4, rest, doppler_bins // 2), f32),
+            pltpu.SemaphoreType.DMA((len(inputs),)),
+            pltpu.SemaphoreType.DMA((4,)),
         ],
         compiler_params=pltpu.CompilerParams(vmem_limit_bytes=KERNEL_VMEM),
         name="azimuth_focus",
-    )(
-        received,
-        reconstruction.reshape(2, channels * channels, pulses),
-        delays,
-        split_constant(to_doppler),
-        halo_doppler,
-        split_constant(final),
-        cosine,
-        sine,
-        reach,
-        square,
-    )
+    )(*inputs)
 
 
 def local(raw_echoes, chirp_spectrum, reconstruction, *rest):

time: 43.1 us -> 53.3 us (1.24)
  Pallas kernels: 42.9 us -> 53.1 us
    pallas_call x1, Pallas kernels: 9.12 us -> 15.2 us  [blocked_local(): pl.pallas_call(functools.partial(azimuth_kernel, (devices, local_pulses,...]
    pallas_call x1, Pallas kernels: 33.8 us -> 38 us  [blocked_local(): pl.pallas_call(functools.partial(compress_kernel, (local_pulses, channels...]
where the time goes in v3:
time: 53.3 us; the launch traced here: 53.1 us
  Pallas kernels  53.1 us (100%)
    pallas_call x1, Pallas kernels, blocked_local(): pl.pallas_call(functools.partial(compress_kernel, (local_pulses, channels...  38 us
    pallas_call x1, Pallas kernels, blocked_local(): pl.pallas_call(functools.partial(azimuth_kernel, (devices, local_pulses,...  15.2 us

profile of v3, /device:TPU:0, one launch (start us, length us, event | category | flops | bytes accessed | tf_op | source)
XLA Modules:
  0.0 53.1 jit_solution(594954172844092672)
XLA Ops:
  0.0 38.0 %compress_exchange.1 = (f32[32,32,128]{2,1,0:T(8,128)}, f32[32,4,128]{2,1,0:T(4,128)}, f32[144,512]{1,0:T(8,128)}, f32[144,512]{1,0:T(8,128)}, s32[144,512]{1,0:...) custom-call(f32[16,128,128]{2,1,0:T(8,128)} %bitcast.16, ...), custom_call_target="tpu_custom_call" | custom-call | tf_op jit(solution)/shard_map/compress_exchange/pallas_call | solution.py:878
  38.0 15.2 %azimuth_focus.1 = f32[2,256,512]{2,1,0:T(8,128)} custom-call(f32[32,32,128]{2,1,0:T(8,128)} %get-tuple-element.14.late_hbm, f32[128,128]{1,0:T(8,128)} %bitcast.18, f32[144,512]{1,0:T(8,128)} %get-tuple-element.16.cos_hbm, f32[144,512]{1,0:T(8,128)} %get-tuple-element.17.sin_hbm, s32[144,512]{1,0:T(8,128)} %get-tuple-element.18.reach_hbm, ...), custom_call_target="tpu_custom_call" | custom-call | tf_op jit(solution)/shard_map/azimuth_focus/pallas_call | solution.py:915

commit v4 on v3

--- a/solution.py
+++ b/solution.py
@@ -528,7 +528,6 @@
             pl.semaphore_wait(barrier, devices - 1)
             send(0)
     send(1)
-    send(2)
     load_halo.wait()
     w = dot_left(halo_ref, jnp.concatenate(packs, axis=1))
     row = lax.broadcasted_iota(jnp.int32, (devices * HALO_ROWS, LANES), 0) % HALO_ROWS
@@ -536,7 +535,6 @@
     for g in range(1, groups):
         total = jnp.where(row // 2 == g, w[:, g * LANES : (g + 1) * LANES], total)
     send_halo_ref[...] = total.reshape(devices, HALO_ROWS, LANES)[:, : 2 * groups, :]
-    send(3)
     own = [
         pltpu.make_async_copy(
             send_ref.at[mine, pl.ds(0, half_rows)], early_ref.at[mine], local_sems.at[0]
@@ -616,6 +614,13 @@
 
         lax.fori_loop(0, devices - 1, body, 0)
 
+    def follow(i, carry):
+        remote(1, i).wait_send()
+        remote(2, i).start()
+        remote(3, i).start()
+        return carry
+
+    lax.fori_loop(0, devices - 1, follow, 0)
     load_doppler.wait()
     own[0].wait()
     arrived((0, 1))
@@ -635,7 +640,7 @@
     arrived((2, 3))
 
     def sent(i, carry):
-        for chunk in range(4):
+        for chunk in (0, 2, 3):
             remote(chunk, i).wait_send()
         return carry
 
@@ -673,6 +678,7 @@
     unfolded,
     focused,
     image_ref,
+    early_image_ref,
     load_sems,
     store_sems,
 ):
@@ -701,10 +707,15 @@
         load(sin_hbm, sin_ref),
     ]
     load_final = load(final_hbm, final_ref)
-    passed = load(image_hbm, out_hbm.at[:, pl.ds(0, ready)])
+    load_image = load(image_hbm, early_image_ref)
 
     load_doppler.wait()
     load_late.wait()
+    load_image.wait()
+    passed = pltpu.make_async_copy(
+        early_image_ref, out_hbm.at[:, pl.ds(0, ready)], store_sems.at[4]
+    )
+    passed.start()
     half = LANES
     flat = late_ref.reshape(sources * pulses * 8, LANES)
     for c in range(channels):
@@ -923,8 +934,9 @@
             pltpu.VMEM((rest + MIG, 2 * doppler_bins), f32),
             pltpu.VMEM((rest, 2 * doppler_bins), f32),
             pltpu.VMEM((4, rest, doppler_bins // 2), f32),
+            pltpu.VMEM((2, ready, doppler_bins), f32),
             pltpu.SemaphoreType.DMA((len(inputs),)),
-            pltpu.SemaphoreType.DMA((4,)),
+            pltpu.SemaphoreType.DMA((5,)),
         ],
         compiler_params=pltpu.CompilerParams(vmem_limit_bytes=KERNEL_VMEM),
         name="azimuth_focus",

time: 53.3 us -> 43.9 us (0.82)
  Pallas kernels: 53.1 us -> 43.8 us
    pallas_call x1, Pallas kernels: 15.2 us -> 7.35 us  [blocked_local(): pl.pallas_call(functools.partial(azimuth_kernel, (devices, local_pulses,...]
    pallas_call x1, Pallas kernels: 38 us -> 36.4 us  [blocked_local(): pl.pallas_call(functools.partial(compress_kernel, (local_pulses, channels...]
where the time goes in v4:
time: 43.9 us; the launch traced here: 43.8 us
  Pallas kernels  43.8 us (100%)
    pallas_call x1, Pallas kernels, blocked_local(): pl.pallas_call(functools.partial(compress_kernel, (local_pulses, channels...  36.4 us
    pallas_call x1, Pallas kernels, blocked_local(): pl.pallas_call(functools.partial(azimuth_kernel, (devices, local_pulses,...  7.35 us

profile of v4, /device:TPU:0, one launch (start us, length us, event | category | flops | bytes accessed | tf_op | source)
XLA Modules:
  0.0 43.8 jit_solution(16440730943904688352)
XLA Ops:
  0.0 36.4 %compress_exchange.1 = (f32[32,32,128]{2,1,0:T(8,128)}, f32[32,4,128]{2,1,0:T(4,128)}, f32[144,512]{1,0:T(8,128)}, f32[144,512]{1,0:T(8,128)}, s32[144,512]{1,0:...) custom-call(f32[16,128,128]{2,1,0:T(8,128)} %bitcast.16, ...), custom_call_target="tpu_custom_call" | custom-call | tf_op jit(solution)/shard_map/compress_exchange/pallas_call | solution.py:889
  36.4 7.3 %azimuth_focus.1 = f32[2,256,512]{2,1,0:T(8,128)} custom-call(f32[32,32,128]{2,1,0:T(8,128)} %get-tuple-element.14.late_hbm, f32[128,128]{1,0:T(8,128)} %bitcast.18, f32[144,512]{1,0:T(8,128)} %get-tuple-element.16.cos_hbm, f32[144,512]{1,0:T(8,128)} %get-tuple-element.17.sin_hbm, s32[144,512]{1,0:T(8,128)} %get-tuple-element.18.reach_hbm, ...), custom_call_target="tpu_custom_call" | custom-call | tf_op jit(solution)/shard_map/azimuth_focus/pallas_call | solution.py:926

commit v5 on v2

--- a/solution.py
+++ b/solution.py
@@ -254,6 +254,115 @@
     )
 
 
+def dot_exact(values, matrix):
+    high = values.astype(jnp.bfloat16)
+    rest = values - high.astype(jnp.float32)
+    middle = rest.astype(jnp.bfloat16)
+    low = (rest - middle.astype(jnp.float32)).astype(jnp.bfloat16)
+    return dot(high, matrix) + dot(middle, matrix) + dot(low, matrix)
+
+
+def doppler_of(lane):
+    return (lane % (LANES // 4)) * 4 + lane // (LANES // 4)
+
+
+def mix_channels(spectra, mix, unfolded, rows, shift):
+    channels = spectra.shape[0]
+    pulses = spectra.shape[2] // 2
+    length = channels * pulses
+
+    def mix_rows(index, carry):
+        at = pl.ds(pl.multiple_of(index * 8, 8), 8)
+        to = pl.ds(pl.multiple_of(index * 8 + shift, 8), 8)
+        spec = [spectra[c, at, :] for c in range(channels)]
+        for b in range(channels):
+            total_r = total_i = None
+            for c in range(channels):
+                m = b * channels + c
+                m_r = jnp.broadcast_to(mix[0, m : m + 1, :], (8, pulses))
+                m_i = jnp.broadcast_to(mix[1, m : m + 1, :], (8, pulses))
+                d_r, d_i = spec[c][:, :pulses], spec[c][:, pulses:]
+                r = m_r * d_r - m_i * d_i
+                i = m_r * d_i + m_i * d_r
+                total_r = r if c == 0 else total_r + r
+                total_i = i if c == 0 else total_i + i
+            unfolded[to, b * pulses : (b + 1) * pulses] = total_r
+            unfolded[to, length + b * pulses : length + (b + 1) * pulses] = total_i
+        return carry
+
+    lax.fori_loop(0, rows // 8, mix_rows, 0)
+
+
+def migrate_rows(unfolded, cos_ref, sin_ref, reach_ref, square_ref, focused, rows):
+    length = reach_ref.shape[1]
+
+    def focus_band(b, carry):
+        lane = pl.multiple_of(b * LANES, LANES)
+        at_real = pl.ds(lane, LANES)
+        at_imag = pl.ds(pl.multiple_of(length + lane, LANES), LANES)
+        for start in range(0, rows, 8):
+            at = slice(start, start + 8)
+            band_square = square_ref[at, :]
+            reach = reach_ref[at, at_real]
+            real = unfolded[at, at_real]
+            imag = unfolded[at, at_imag]
+            bound = band_square
+            for offset in range(1, MIG + 1):
+                moved = reach >= bound
+                window = slice(start + offset, start + offset + 8)
+                real = jnp.where(moved, unfolded[window, at_real], real)
+                imag = jnp.where(moved, unfolded[window, at_imag], imag)
+                bound = bound + band_square
+            cosine = cos_ref[at, at_real]
+            sine = sin_ref[at, at_real]
+            focused[at, at_real] = real * cosine - imag * sine
+            focused[at, at_imag] = real * sine + imag * cosine
+        return carry
+
+    lax.fori_loop(0, length // LANES, focus_band, 0)
+
+
+def inverse_rows(focused, final_ref, twiddle_ref, at):
+    group = LANES // 4
+    rows = at.stop - at.start
+    line = lax.broadcasted_iota(jnp.int32, (rows, LANES), 1) // group
+    parts = []
+    for part in range(2):
+        base = part * 4 * LANES
+        turned = []
+        for b in range(4):
+            value = focused[at, base + b * LANES : base + (b + 1) * LANES]
+            turned.append(value if b == 0 else pltpu.roll(value, b * group, 1))
+        grouped = []
+        for j in range(4):
+            value = turned[(0 - j) % 4]
+            for g in range(1, 4):
+                value = jnp.where(line == g, turned[(g - j) % 4], value)
+            grouped.append(value if j == 0 else pltpu.roll(value, LANES - j * group, 1))
+        parts.append(grouped)
+    stacked = jnp.concatenate(
+        [jnp.concatenate([parts[0][j], parts[1][j]], axis=1) for j in range(4)], axis=0
+    )
+    image = dot_right(stacked, final_ref)
+    real, imag = [], []
+    for j in range(4):
+        r = image[j * rows : (j + 1) * rows, :LANES]
+        i = image[j * rows : (j + 1) * rows, LANES:]
+        if j > 0:
+            t_r, t_i = twiddle_ref[0, j : j + 1, :], twiddle_ref[1, j : j + 1, :]
+            r, i = r * t_r - i * t_i, r * t_i + i * t_r
+        real.append(r)
+        imag.append(i)
+    a_r, a_i = real[0] + real[2], imag[0] + imag[2]
+    b_r, b_i = real[0] - real[2], imag[0] - imag[2]
+    c_r, c_i = real[1] + real[3], imag[1] + imag[3]
+    d_r, d_i = imag[3] - imag[1], real[1] - real[3]
+    return (
+        jnp.concatenate([a_r + c_r, b_r + d_r, a_r - c_r, b_r - d_r], axis=1),
+        jnp.concatenate([a_i + c_i, b_i + d_i, a_i - c_i, b_i - d_i], axis=1),
+    )
+
+
 def compress_kernel(
     sizes,
     x_hbm,
@@ -267,11 +376,15 @@
     inv_hbm,
     last_hbm,
     halo_hbm,
+    reconstruction_hbm,
+    delays_hbm,
+    order_hbm,
     recv_ref,
     cos_hbm,
     sin_hbm,
     reach_hbm,
     square_hbm,
+    mix_hbm,
     x_ref,
     chirp_ref,
     rate_ref,
@@ -283,12 +396,16 @@
     inv_ref,
     last_ref,
     halo_ref,
+    reconstruction_ref,
+    delays_ref,
+    order_ref,
     send_ref,
     rows_ref,
     cos_ref,
     sin_ref,
     reach_ref,
     square_ref,
+    mix_ref,
     load_sems,
     store_sems,
     local_sem,
@@ -335,6 +452,9 @@
     load_rate = start_load(rate_hbm, rate_ref)
     load_band = start_load(band_hbm, band_ref)
     load_migration = start_load(migration_hbm, migration_ref)
+    load_reconstruction = start_load(reconstruction_hbm, reconstruction_ref)
+    load_delays = start_load(delays_hbm, delays_ref)
+    load_order = start_load(order_hbm, order_ref)
     lax.fori_loop(1, devices, greet, 0)
 
     rows = pulses * channels * 4 + HALO_ROWS
@@ -438,6 +558,24 @@
     own = pltpu.make_async_copy(send_ref.at[mine], recv_ref.at[mine], local_sem)
     own.start()
 
+    load_reconstruction.wait()
+    load_delays.wait()
+    load_order.wait()
+    bins_f = pulses * devices
+    shape = (channels * channels, bins_f)
+    row = lax.broadcasted_iota(jnp.int32, shape, 0) % channels
+    frequency = doppler_of(lax.broadcasted_iota(jnp.int32, shape, 1))
+    delay = jnp.zeros_like(row)
+    for c in range(channels):
+        one = jnp.broadcast_to(delays_ref[0:1, c : c + 1], row.shape)
+        delay = jnp.where(row == c, one, delay)
+    turns = lax.rem(frequency * delay, bins_f).astype(jnp.float32) * (1.0 / bins_f)
+    align_r, align_i = cos_sin_turns(turns)
+    rec_r = dot_exact(reconstruction_ref[0], order_ref[...])
+    rec_i = dot_exact(reconstruction_ref[1], order_ref[...])
+    mix_ref[0] = rec_r * align_r - rec_i * align_i
+    mix_ref[1] = rec_r * align_i + rec_i * align_r
+
     load_rate.wait()
     load_band.wait()
     load_migration.wait()
@@ -454,7 +592,7 @@
         band_square = band * band
         square_ref[at, :] = band_square
         for start in range(0, length, LANES):
-            doppler = lax.broadcasted_iota(jnp.int32, (8, LANES), 1) + start
+            doppler = doppler_of(lax.broadcasted_iota(jnp.int32, (8, LANES), 1)) + start
             centred = jnp.where(doppler >= length // 2, doppler - length, doppler)
             relative = centred.astype(jnp.float32) * (2.0 / length)
             cosine, sine = cos_sin_turns(rate * (relative * relative * (curvature / 2.0)))
@@ -474,6 +612,7 @@
         (sin_ref, sin_hbm),
         (reach_ref, reach_hbm),
         (square_ref, square_hbm),
+        (mix_ref, mix_hbm),
     ):
         copy = pltpu.make_async_copy(source, target, store_sems.at[len(stores)])
         copy.start()
@@ -495,33 +634,36 @@
 def azimuth_kernel(
     sizes,
     recv_hbm,
-    reconstruction_ref,
-    delays_ref,
+    doppler_hbm,
+    halo_doppler_hbm,
+    mix_hbm,
+    reach_hbm,
+    square_hbm,
+    cos_hbm,
+    sin_hbm,
+    final_hbm,
+    twiddle_hbm,
+    out_hbm,
+    recv_ref,
     doppler_ref,
     halo_doppler_ref,
-    final_hbm,
-    cos_hbm,
-    sin_hbm,
-    reach_hbm,
-    square_hbm,
-    out_ref,
-    recv_ref,
+    mix_ref,
+    reach_ref,
+    square_ref,
+    cos_ref,
+    sin_ref,
+    final_ref,
+    twiddle_ref,
     spectra,
     unfolded,
     focused,
-    mix,
-    final,
-    cos_ref,
-    sin_ref,
-    reach_ref,
-    square_ref,
+    image_ref,
     load_sems,
     recv_sems,
+    store_sems,
 ):
     sources, local_pulses, channels, bins = sizes
-    pulses = sources * local_pulses
     block = local_pulses * channels * 4 + HALO_ROWS
-    length = channels * pulses
     arrivals = []
 
     def arrive(row):
@@ -532,37 +674,35 @@
         copy.start()
         arrivals.append(copy)
 
+    loads = []
+
+    def load(source, target):
+        copy = pltpu.make_async_copy(source, target, load_sems.at[len(loads)])
+        copy.start()
+        loads.append(copy)
+        return copy
+
+    load_doppler = load(doppler_hbm, doppler_ref)
     for pair in range(channels // 2):
         for p in range(local_pulses):
             arrive((p * (channels // 2) + pair) * 8)
     arrive(local_pulses * channels * 4)
-    loads = []
-    for source, target in (
-        (reach_hbm, reach_ref),
-        (square_hbm, square_ref),
-        (cos_hbm, cos_ref),
-        (sin_hbm, sin_ref),
-        (final_hbm, final),
-    ):
-        copy = pltpu.make_async_copy(source, target, load_sems.at[len(loads)])
-        copy.start()
-        loads.append(copy)
-
-    row = lax.broadcasted_iota(jnp.int32, (channels * channels, pulses), 0) % channels
-    frequency = lax.broadcasted_iota(jnp.int32, (channels * channels, pulses), 1)
-    delay = jnp.zeros_like(row)
-    for c in range(channels):
-        delay = jnp.where(row == c, delays_ref[c], delay)
-    turns = lax.rem(frequency * delay, pulses).astype(jnp.float32) * (1.0 / pulses)
-    align_r, align_i = cos_sin_turns(turns)
-    rec_r, rec_i = reconstruction_ref[0], reconstruction_ref[1]
-    mix[0] = rec_r * align_r - rec_i * align_i
-    mix[1] = rec_r * align_i + rec_i * align_r
+    load_halo_doppler = load(halo_doppler_hbm, halo_doppler_ref)
+    load_mix = load(mix_hbm, mix_ref)
+    load_tables = [
+        load(reach_hbm, reach_ref),
+        load(square_hbm, square_ref),
+        load(cos_hbm, cos_ref),
+        load(sin_hbm, sin_ref),
+    ]
+    load_final = [load(final_hbm, final_ref), load(twiddle_hbm, twiddle_ref)]
+
+    flat = recv_ref.reshape(sources * block, LANES)
 
     def rows_of(start):
         return flat[pl.ds(start, sources, stride=block), :]
 
-    flat = recv_ref.reshape(sources * block, LANES)
+    load_doppler.wait()
     for c in range(channels):
         if c % 2 == 0:
             for p in range(local_pulses):
@@ -580,13 +720,9 @@
     groups = local_pulses * channels * MIG // LANES
     per_group = LANES // (MIG * channels)
     arrivals[-1].wait()
+    load_halo_doppler.wait()
     h = jnp.concatenate(
-        [
-            rows_of(local_pulses * channels * 4 + g * 2 + part)
-            for g in range(groups)
-            for part in range(2)
-        ],
-        axis=0,
+        [rows_of(local_pulses * channels * 4 + j) for j in range(2 * groups)], axis=0
     ).T
     step = channels * MIG
     halo = dot_right(h[:step], halo_doppler_ref.at[0])
@@ -594,58 +730,27 @@
         halo = halo + dot_right(h[k * step : (k + 1) * step], halo_doppler_ref.at[k])
     for c in range(channels):
         spectra[c, bins:, :] = halo[c * MIG : (c + 1) * MIG]
-
-    def mix_rows(index, carry):
-        at = pl.ds(pl.multiple_of(index * 8, 8), 8)
-        spec = [spectra[c, at, :] for c in range(channels)]
-        for b in range(channels):
-            total_r = total_i = None
-            for c in range(channels):
-                m = b * channels + c
-                m_r = jnp.broadcast_to(mix[0, m : m + 1, :], (8, pulses))
-                m_i = jnp.broadcast_to(mix[1, m : m + 1, :], (8, pulses))
-                d_r, d_i = spec[c][:, :pulses], spec[c][:, pulses:]
-                r = m_r * d_r - m_i * d_i
-                i = m_r * d_i + m_i * d_r
-                total_r = r if c == 0 else total_r + r
-                total_i = i if c == 0 else total_i + i
-            unfolded[at, b * pulses : (b + 1) * pulses] = total_r
-            unfolded[at, length + b * pulses : length + (b + 1) * pulses] = total_i
-        return carry
-
-    lax.fori_loop(0, (bins + MIG) // 8, mix_rows, 0)
-
-    for copy in loads[:-1]:
+    load_mix.wait()
+    mix_channels(spectra, mix_ref, unfolded, bins + MIG, 0)
+    for copy in load_tables:
         copy.wait()
-
-    def focus_band(b, carry):
-        lane = pl.multiple_of(b * LANES, LANES)
-        at_real = pl.ds(lane, LANES)
-        at_imag = pl.ds(pl.multiple_of(length + lane, LANES), LANES)
-        for start in range(0, bins, 8):
-            at = slice(start, start + 8)
-            band_square = square_ref[at, :]
-            reach = reach_ref[at, at_real]
-            real = unfolded[at, at_real]
-            imag = unfolded[at, at_imag]
-            bound = band_square
-            for offset in range(1, MIG + 1):
-                moved = reach >= bound
-                window = slice(start + offset, start + offset + 8)
-                real = jnp.where(moved, unfolded[window, at_real], real)
-                imag = jnp.where(moved, unfolded[window, at_imag], imag)
-                bound = bound + band_square
-            cosine = cos_ref[at, at_real]
-            sine = sin_ref[at, at_real]
-            focused[at, at_real] = real * cosine - imag * sine
-            focused[at, at_imag] = real * sine + imag * cosine
-        return carry
-
-    lax.fori_loop(0, length // LANES, focus_band, 0)
-    loads[-1].wait()
-    image = dot_right(focused[...], final)
-    out_ref[0] = image[:, :length]
-    out_ref[1] = image[:, length:]
+    migrate_rows(unfolded, cos_ref, sin_ref, reach_ref, square_ref, focused, bins)
+    for copy in load_final:
+        copy.wait()
+    stores = []
+    for k in range(bins // LANES):
+        at = slice(k * LANES, (k + 1) * LANES)
+        real, imag = inverse_rows(focused, final_ref, twiddle_ref, at)
+        image_ref[0, at, :] = real
+        image_ref[1, at, :] = imag
+        rows = pl.ds(k * LANES, LANES)
+        copy = pltpu.make_async_copy(
+            image_ref.at[:, rows], out_hbm.at[:, rows], store_sems.at[k]
+        )
+        copy.start()
+        stores.append(copy)
+    for copy in stores:
+        copy.wait()
 
 
 def fits(pulses, channels, length, devices):
@@ -657,7 +762,7 @@
         pulses == LANES
         and length % (LANES * devices) == 0
         and bins == 2 * LANES
-        and channels % 2 == 0
+        and channels == 4
         and 2 * lead == LANES
         and devices % 8 == 0
         and signals * MIG % LANES == 0
@@ -708,7 +813,8 @@
     twiddles = np.stack(roots(leads, lanes, length, -1.0)).astype(np.float32)
 
     sources = np.arange(devices)
-    bins_f = np.arange(pulses)
+    bins_f = doppler_of(np.arange(pulses))
+    order_f = (np.arange(pulses)[:, None] == bins_f[None, :]).astype(ml_dtypes.bfloat16)
     order = (np.arange(local_pulses)[:, None] + sources[None, :] * local_pulses).reshape(-1)
     scale = 1.0 / math.sqrt(pulses)
     to_doppler = right_matrix(*roots(order, bins_f, pulses, -1.0)) * scale
@@ -726,9 +832,9 @@
             )
         halo_doppler.append(split_constant(np.concatenate(by_group, axis=0)))
     halo_doppler = np.stack(halo_doppler)
-    indices = np.arange(doppler_bins)
-    final = right_matrix(*roots(indices, indices, doppler_bins, 1.0)) / math.sqrt(doppler_bins)
-    final = final.reshape(2 * doppler_bins, 2 * doppler_bins)
+    final = right_matrix(*roots(lanes, lanes, LANES, 1.0)) / math.sqrt(doppler_bins)
+    final = split_constant(final.reshape(2 * LANES, 2 * LANES))
+    regroup = np.stack(roots(np.arange(8) % 4, lanes, doppler_bins, 1.0)).astype(np.float32)
 
     x = raw_echoes.reshape(signals, 2, lead, LANES).transpose(0, 2, 1, 3)
     x = x.reshape(signals, 2 * lead, LANES)
@@ -748,8 +854,11 @@
         split_constant(inverse),
         split_constant(pair),
         split_constant(halo),
-    )
-    received, cosine, sine, reach, square = pl.pallas_call(
+        reconstruction.reshape(2, channels * channels, pulses),
+        delays.reshape(1, channels),
+        order_f,
+    )
+    received, cosine, sine, reach, square, mix = pl.pallas_call(
         functools.partial(
             compress_kernel, (local_pulses, channels, lead, devices, inner, doppler_bins)
         ),
@@ -759,9 +868,10 @@
             jax.ShapeDtypeStruct(tables, jnp.float32),
             jax.ShapeDtypeStruct(tables, jnp.int32),
             jax.ShapeDtypeStruct((bins, LANES), jnp.int32),
+            jax.ShapeDtypeStruct((2, channels * channels, pulses), jnp.float32),
         ),
         in_specs=[hbm()] * len(operands),
-        out_specs=(hbm(),) * 5,
+        out_specs=(hbm(),) * 6,
         scratch_shapes=[pltpu.VMEM(value.shape, value.dtype) for value in operands]
         + [
             pltpu.VMEM((devices, block, LANES), jnp.float32),
@@ -770,8 +880,9 @@
             pltpu.VMEM(tables, jnp.float32),
             pltpu.VMEM(tables, jnp.int32),
             pltpu.VMEM((bins, LANES), jnp.int32),
+            pltpu.VMEM((2, channels * channels, pulses), jnp.float32),
             pltpu.SemaphoreType.DMA((len(operands) + local_pulses - 1,)),
-            pltpu.SemaphoreType.DMA((4,)),
+            pltpu.SemaphoreType.DMA((5,)),
             pltpu.SemaphoreType.DMA,
             pltpu.SemaphoreType.DMA((2, devices)),
             pltpu.SemaphoreType.DMA((2, devices)),
@@ -781,50 +892,36 @@
         ),
         name="compress_exchange",
     )(*operands)
+    inputs = (
+        received,
+        split_constant(to_doppler),
+        halo_doppler,
+        mix,
+        reach,
+        square,
+        cosine,
+        sine,
+        final,
+        regroup,
+    )
     return pl.pallas_call(
         functools.partial(azimuth_kernel, (devices, local_pulses, channels, bins)),
         out_shape=jax.ShapeDtypeStruct((2, bins, doppler_bins), jnp.float32),
-        in_specs=[
-            hbm(),
-            vmem(),
-            pl.BlockSpec(memory_space=pltpu.SMEM),
-            vmem(),
-            vmem(),
-            hbm(),
-            hbm(),
-            hbm(),
-            hbm(),
-            hbm(),
-        ],
-        out_specs=vmem(),
-        scratch_shapes=[
-            pltpu.VMEM((devices, block, LANES), jnp.float32),
+        in_specs=[hbm()] * len(inputs),
+        out_specs=hbm(),
+        scratch_shapes=[pltpu.VMEM(value.shape, value.dtype) for value in inputs]
+        + [
             pltpu.VMEM((channels, bins + MIG, 2 * pulses), jnp.float32),
             pltpu.VMEM((bins + MIG, 2 * doppler_bins), jnp.float32),
             pltpu.VMEM((bins, 2 * doppler_bins), jnp.float32),
-            pltpu.VMEM((2, channels * channels, pulses), jnp.float32),
-            pltpu.VMEM((2, 2 * doppler_bins, 2 * doppler_bins), jnp.bfloat16),
-            pltpu.VMEM(tables, jnp.float32),
-            pltpu.VMEM(tables, jnp.float32),
-            pltpu.VMEM(tables, jnp.int32),
-            pltpu.VMEM((bins, LANES), jnp.int32),
-            pltpu.SemaphoreType.DMA((5,)),
+            pltpu.VMEM((2, bins, doppler_bins), jnp.float32),
+            pltpu.SemaphoreType.DMA((len(inputs) - 1,)),
             pltpu.SemaphoreType.DMA((channels // 2 * local_pulses + 1,)),
+            pltpu.SemaphoreType.DMA((bins // LANES,)),
         ],
         compiler_params=pltpu.CompilerParams(vmem_limit_bytes=KERNEL_VMEM),
         name="azimuth_focus",
-    )(
-        received,
-        reconstruction.reshape(2, channels * channels, pulses),
-        delays,
-        split_constant(to_doppler),
-        halo_doppler,
-        split_constant(final),
-        cosine,
-        sine,
-        reach,
-        square,
-    )
+    )(*inputs)
 
 
 def local(raw_echoes, chirp_spectrum, reconstruction, *rest):

time: 43.1 us -> 41.3 us (0.958)
  Pallas kernels: 42.9 us -> 41.1 us
    pallas_call x1, Pallas kernels: 9.12 us -> 7.28 us  [blocked_local(): pl.pallas_call(functools.partial(azimuth_kernel, (devices, local_pulses,...]
where the time goes in v5:
time: 41.3 us; the launch traced here: 41.1 us
  Pallas kernels  41.1 us (100%)
    pallas_call x1, Pallas kernels, blocked_local(): pl.pallas_call(functools.partial(compress_kernel, (local_pulses, channels...  33.8 us
    pallas_call x1, Pallas kernels, blocked_local(): pl.pallas_call(functools.partial(azimuth_kernel, (devices, local_pulses,...  7.28 us

profile of v5, /device:TPU:0, one launch (start us, length us, event | category | flops | bytes accessed | tf_op | source)
XLA Modules:
  0.0 41.1 jit_solution(6964808555016389610)
XLA Ops:
  0.0 33.8 %compress_exchange.1 = (f32[32,72,128]{2,1,0:T(8,128)}, f32[256,512]{1,0:T(8,128)}, f32[256,512]{1,0:T(8,128)}, s32[256,512]{1,0:T(8,128)}, s32[256,128]{1,0:T(8,128)}, /*index=5*/f32[2,16,128]{2,1,0:T(8,128)}) custom-call(f32[16,128,128]{2,1,0:T(8,128)} %bitcast.15, f32[128,128]{1,0:T(8,128)} %bitcast.16, f32[2,128]{1,0:T(2,128)} %bitcast.18, ...), custom_call_target="tpu_custom_call" | custom-call | tf_op jit(solution)/shard_map/compress_exchange/pallas_call | solution.py:861
  33.9 7.3 %azimuth_focus.1 = f32[2,256,512]{2,1,0:T(8,128)} custom-call(f32[32,72,128]{2,1,0:T(8,128)} %get-tuple-element.11.recv_hbm, bf16[2,256,256]{2,1,0:T(8,128)(2,1)} %constant.29.clone.doppler_hbm, bf16[2,2,128,256]{3,2,1,0:T(8,128)(2,1)} %constant.30.clone.halo_doppler_hbm, f32[2,16,128]{2,1,0:T(8,128)} %get-tuple-element.12.mix_hbm, ...), custom_call_target="tpu_custom_call" | custom-call | tf_op jit(solution)/shard_map/azimuth_focus/pallas_call | solution.py:907

commit v6 on v5

--- a/solution.py
+++ b/solution.py
@@ -459,27 +459,48 @@
 
     rows = pulses * channels * 4 + HALO_ROWS
     cut = channels * 4
-
-    def remote(chunk, i):
-        far = lax.div(i + 1, 2)
-        step = devices // 2 + far - 2 * far * lax.rem(i, 2)
-        target = lax.rem(mine + step, devices)
-        at = pl.ds(0, cut) if chunk == 0 else pl.ds(cut, rows - cut)
+    middle = devices // 2
+
+    def flipped(value, mask):
+        result = value
+        bit = 1
+        while bit <= mask:
+            if mask & bit:
+                result = result + bit * (1 - 2 * lax.rem(lax.div(value, bit), 2))
+            bit *= 2
+        return result
+
+    outer = devices // inner
+    outer_at = [flipped(lax.axis_index("az"), mask) for mask in range(outer)]
+    inner_at = [flipped(lax.axis_index("rg"), mask) for mask in range(inner)]
+
+    def remote(chunk, step):
+        place_outer, place_inner = outer_at[step // inner], inner_at[step % inner]
+        target = place_outer * inner + place_inner
+        if step < middle:
+            at = pl.ds(0, rows)
+        else:
+            at = pl.ds(0, cut) if chunk == 0 else pl.ds(cut, rows - cut)
         return pltpu.make_async_remote_copy(
             src_ref=send_ref.at[target, at],
             dst_ref=recv_ref.at[mine, at],
             send_sem=send_sems.at[chunk, step],
             recv_sem=recv_sems.at[chunk, step],
-            device_id=place(target),
+            device_id=(place_outer, place_inner),
             device_id_type=pl.DeviceIdType.MESH,
         )
 
+    across = range(devices - 1, middle - 1, -1)
+    sequence = [(0, step) for step in across]
+    for step in across:
+        sequence.append((1, step))
+        if step > middle:
+            sequence.append((1, step - middle))
+
     def send(chunk):
-        def body(i, carry):
-            remote(chunk, i).start()
-            return carry
-
-        lax.fori_loop(0, devices - 1, body, 0)
+        for at, step in sequence:
+            if at == chunk:
+                remote(at, step).start()
 
     lane = lax.broadcasted_iota(jnp.int32, (2 * lead, LANES), 1)
     groups = pulses * channels * MIG // LANES
@@ -621,14 +642,10 @@
         copy.wait()
     own.wait()
 
-    def finish(i, carry):
-        for chunk in range(2):
-            copy = remote(chunk, i)
-            copy.wait_send()
-            copy.wait_recv()
-        return carry
-
-    lax.fori_loop(0, devices - 1, finish, 0)
+    for chunk, step in sequence:
+        copy = remote(chunk, step)
+        copy.wait_send()
+        copy.wait_recv()
 
 
 def azimuth_kernel(
@@ -765,6 +782,7 @@
         and channels == 4
         and 2 * lead == LANES
         and devices % 8 == 0
+        and devices & (devices - 1) == 0
         and signals * MIG % LANES == 0
         and LANES % (MIG * channels) == 0
         and 2 * (signals * MIG // LANES) <= HALO_ROWS

time: 41.3 us -> 42.7 us (1.034)
  Pallas kernels: 41.1 us -> 42.5 us
    pallas_call x1, Pallas kernels: 33.8 us -> 35.2 us  [blocked_local(): pl.pallas_call(functools.partial(compress_kernel, (local_pulses, channels...]
where the time goes in v6:
time: 42.7 us; the launch traced here: 42.5 us
  Pallas kernels  42.5 us (100%)
    pallas_call x1, Pallas kernels, blocked_local(): pl.pallas_call(functools.partial(compress_kernel, (local_pulses, channels...  35.2 us
    pallas_call x1, Pallas kernels, blocked_local(): pl.pallas_call(functools.partial(azimuth_kernel, (devices, local_pulses,...  7.28 us

profile of v6, /device:TPU:0, one launch (start us, length us, event | category | flops | bytes accessed | tf_op | source)
XLA Modules:
  0.0 42.5 jit_solution(17188349745945829436)
XLA Ops:
  0.0 35.2 %compress_exchange.1 = (f32[32,72,128]{2,1,0:T(8,128)}, f32[256,512]{1,0:T(8,128)}, f32[256,512]{1,0:T(8,128)}, s32[256,512]{1,0:T(8,128)}, s32[256,128]{1,0:T(8,128)}, /*index=5*/f32[2,16,128]{2,1,0:T(8,128)}) custom-call(f32[16,128,128]{2,1,0:T(8,128)} %bitcast.15, f32[128,128]{1,0:T(8,128)} %bitcast.16, f32[2,128]{1,0:T(2,128)} %bitcast.18, ...), custom_call_target="tpu_custom_call" | custom-call | tf_op jit(solution)/shard_map/compress_exchange/pallas_call | solution.py:879
  35.2 7.3 %azimuth_focus.1 = f32[2,256,512]{2,1,0:T(8,128)} custom-call(f32[32,72,128]{2,1,0:T(8,128)} %get-tuple-element.11.recv_hbm, bf16[2,256,256]{2,1,0:T(8,128)(2,1)} %constant.29.clone.doppler_hbm, bf16[2,2,128,256]{3,2,1,0:T(8,128)(2,1)} %constant.30.clone.halo_doppler_hbm, f32[2,16,128]{2,1,0:T(8,128)} %get-tuple-element.12.mix_hbm, ...), custom_call_target="tpu_custom_call" | custom-call | tf_op jit(solution)/shard_map/azimuth_focus/pallas_call | solution.py:925

commit v7 on v5

--- a/solution.py
+++ b/solution.py
@@ -272,15 +272,14 @@
     length = channels * pulses
 
     def mix_rows(index, carry):
-        at = pl.ds(pl.multiple_of(index * 8, 8), 8)
-        to = pl.ds(pl.multiple_of(index * 8 + shift, 8), 8)
+        at = pl.ds(pl.multiple_of(index * 16, 16), 16)
+        to = pl.ds(pl.multiple_of(index * 16 + shift, 8), 16)
         spec = [spectra[c, at, :] for c in range(channels)]
         for b in range(channels):
             total_r = total_i = None
             for c in range(channels):
                 m = b * channels + c
-                m_r = jnp.broadcast_to(mix[0, m : m + 1, :], (8, pulses))
-                m_i = jnp.broadcast_to(mix[1, m : m + 1, :], (8, pulses))
+                m_r, m_i = mix[0, m : m + 1, :], mix[1, m : m + 1, :]
                 d_r, d_i = spec[c][:, :pulses], spec[c][:, pulses:]
                 r = m_r * d_r - m_i * d_i
                 i = m_r * d_i + m_i * d_r
@@ -290,33 +289,43 @@
             unfolded[to, length + b * pulses : length + (b + 1) * pulses] = total_i
         return carry
 
-    lax.fori_loop(0, rows // 8, mix_rows, 0)
-
-
-def migrate_rows(unfolded, cos_ref, sin_ref, reach_ref, square_ref, focused, rows):
-    length = reach_ref.shape[1]
+    lax.fori_loop(0, rows // 16, mix_rows, 0)
+
+
+def migrate_rows(unfolded, cos_ref, sin_ref, shift_ref, focused, rows):
+    length = shift_ref.shape[1]
 
     def focus_band(b, carry):
         lane = pl.multiple_of(b * LANES, LANES)
-        at_real = pl.ds(lane, LANES)
-        at_imag = pl.ds(pl.multiple_of(length + lane, LANES), LANES)
+        columns = (pl.ds(lane, LANES), pl.ds(pl.multiple_of(length + lane, LANES), LANES))
+
+        def windows(start):
+            return [
+                [unfolded[start + k : start + k + 8, column] for k in range(8)]
+                for column in columns
+            ]
+
+        ahead = windows(0)
         for start in range(0, rows, 8):
             at = slice(start, start + 8)
-            band_square = square_ref[at, :]
-            reach = reach_ref[at, at_real]
-            real = unfolded[at, at_real]
-            imag = unfolded[at, at_imag]
-            bound = band_square
-            for offset in range(1, MIG + 1):
-                moved = reach >= bound
-                window = slice(start + offset, start + offset + 8)
-                real = jnp.where(moved, unfolded[window, at_real], real)
-                imag = jnp.where(moved, unfolded[window, at_imag], imag)
-                bound = bound + band_square
-            cosine = cos_ref[at, at_real]
-            sine = sin_ref[at, at_real]
-            focused[at, at_real] = real * cosine - imag * sine
-            focused[at, at_imag] = real * sine + imag * cosine
+            now, ahead = ahead, windows(start + 8)
+            shift = shift_ref[at, columns[0]]
+            bits = [(shift & (1 << level)) != 0 for level in range(5)]
+            values = []
+            for part, column in enumerate(columns):
+                level_values = now[part] + ahead[part]
+                for level in range(4):
+                    level_values = [
+                        jnp.where(bits[level], level_values[k + 1], level_values[k])
+                        for k in range(0, len(level_values), 2)
+                    ]
+                last = unfolded[start + MIG : start + MIG + 8, column]
+                values.append(jnp.where(bits[4], last, level_values[0]))
+            real, imag = values
+            cosine = cos_ref[at, columns[0]]
+            sine = sin_ref[at, columns[0]]
+            focused[at, columns[0]] = real * cosine - imag * sine
+            focused[at, columns[1]] = real * sine + imag * cosine
         return carry
 
     lax.fori_loop(0, length // LANES, focus_band, 0)
@@ -380,10 +389,10 @@
     delays_hbm,
     order_hbm,
     recv_ref,
+    halo_recv_ref,
     cos_hbm,
     sin_hbm,
-    reach_hbm,
-    square_hbm,
+    shift_hbm,
     mix_hbm,
     x_ref,
     chirp_ref,
@@ -400,15 +409,15 @@
     delays_ref,
     order_ref,
     send_ref,
+    send_halo_ref,
     rows_ref,
     cos_ref,
     sin_ref,
-    reach_ref,
-    square_ref,
+    shift_ref,
     mix_ref,
     load_sems,
     store_sems,
-    local_sem,
+    local_sems,
     send_sems,
     recv_sems,
 ):
@@ -457,17 +466,23 @@
     load_order = start_load(order_hbm, order_ref)
     lax.fori_loop(1, devices, greet, 0)
 
-    rows = pulses * channels * 4 + HALO_ROWS
+    rows = pulses * channels * 4
     cut = channels * 4
+
+    def parts(chunk, target):
+        if chunk == 2:
+            return send_halo_ref.at[target], halo_recv_ref.at[mine]
+        at = pl.ds(0, cut) if chunk == 0 else pl.ds(cut, rows - cut)
+        return send_ref.at[target, at], recv_ref.at[mine, at]
 
     def remote(chunk, i):
         far = lax.div(i + 1, 2)
         step = devices // 2 + far - 2 * far * lax.rem(i, 2)
         target = lax.rem(mine + step, devices)
-        at = pl.ds(0, cut) if chunk == 0 else pl.ds(cut, rows - cut)
+        source, landing = parts(chunk, target)
         return pltpu.make_async_remote_copy(
-            src_ref=send_ref.at[target, at],
-            dst_ref=recv_ref.at[mine, at],
+            src_ref=source,
+            dst_ref=landing,
             send_sem=send_sems.at[chunk, step],
             recv_sem=recv_sems.at[chunk, step],
             device_id=place(target),
@@ -547,16 +562,21 @@
         if p == 0:
             pl.semaphore_wait(barrier, devices - 1)
             send(0)
+    send(1)
     load_halo.wait()
     w = dot_left(halo_ref, jnp.concatenate(packs, axis=1))
     row = lax.broadcasted_iota(jnp.int32, (devices * HALO_ROWS, LANES), 0) % HALO_ROWS
     total = w[:, :LANES]
     for g in range(1, groups):
         total = jnp.where(row // 2 == g, w[:, g * LANES : (g + 1) * LANES], total)
-    send_ref[:, pulses * channels * 4 :, :] = total.reshape(devices, HALO_ROWS, LANES)
-    send(1)
-    own = pltpu.make_async_copy(send_ref.at[mine], recv_ref.at[mine], local_sem)
-    own.start()
+    send_halo_ref[...] = total.reshape(devices, HALO_ROWS, LANES)[:, : 2 * groups, :]
+    send(2)
+    own = [
+        pltpu.make_async_copy(send_ref.at[mine], recv_ref.at[mine], local_sems.at[0]),
+        pltpu.make_async_copy(send_halo_ref.at[mine], halo_recv_ref.at[mine], local_sems.at[1]),
+    ]
+    for copy in own:
+        copy.start()
 
     load_reconstruction.wait()
     load_delays.wait()
@@ -590,7 +610,6 @@
         band = rows_ref[1, at, :].astype(jnp.int32)
         move = rows_ref[2, at, :].astype(jnp.int32)
         band_square = band * band
-        square_ref[at, :] = band_square
         for start in range(0, length, LANES):
             doppler = doppler_of(lax.broadcasted_iota(jnp.int32, (8, LANES), 1)) + start
             centred = jnp.where(doppler >= length // 2, doppler - length, doppler)
@@ -600,9 +619,13 @@
             columns = slice(start, start + LANES)
             cos_ref[at, columns] = jnp.where(inside, cosine, 0.0)
             sin_ref[at, columns] = jnp.where(inside, sine, 0.0)
-            reach_ref[at, columns] = move * jnp.minimum(centred * centred, band_square) + (
-                band_square >> 1
-            )
+            reach = move * jnp.minimum(centred * centred, band_square) + (band_square >> 1)
+            shift = jnp.zeros((8, LANES), jnp.int32)
+            bound = band_square
+            for offset in range(1, MIG + 1):
+                shift = jnp.where(reach >= bound, offset, shift)
+                bound = bound + band_square
+            shift_ref[at, columns] = shift
         return carry
 
     lax.fori_loop(0, bins // 8, tables, 0)
@@ -610,8 +633,7 @@
     for source, target in (
         (cos_ref, cos_hbm),
         (sin_ref, sin_hbm),
-        (reach_ref, reach_hbm),
-        (square_ref, square_hbm),
+        (shift_ref, shift_hbm),
         (mix_ref, mix_hbm),
     ):
         copy = pltpu.make_async_copy(source, target, store_sems.at[len(stores)])
@@ -619,10 +641,11 @@
         stores.append(copy)
     for copy in stores:
         copy.wait()
-    own.wait()
+    for copy in own:
+        copy.wait()
 
     def finish(i, carry):
-        for chunk in range(2):
+        for chunk in range(3):
             copy = remote(chunk, i)
             copy.wait_send()
             copy.wait_recv()
@@ -634,22 +657,22 @@
 def azimuth_kernel(
     sizes,
     recv_hbm,
+    halo_hbm,
     doppler_hbm,
     halo_doppler_hbm,
     mix_hbm,
-    reach_hbm,
-    square_hbm,
+    shift_hbm,
     cos_hbm,
     sin_hbm,
     final_hbm,
     twiddle_hbm,
     out_hbm,
     recv_ref,
+    halo_ref,
     doppler_ref,
     halo_doppler_ref,
     mix_ref,
-    reach_ref,
-    square_ref,
+    shift_ref,
     cos_ref,
     sin_ref,
     final_ref,
@@ -663,7 +686,7 @@
     store_sems,
 ):
     sources, local_pulses, channels, bins = sizes
-    block = local_pulses * channels * 4 + HALO_ROWS
+    block = local_pulses * channels * 4
     arrivals = []
 
     def arrive(row):
@@ -686,12 +709,11 @@
     for pair in range(channels // 2):
         for p in range(local_pulses):
             arrive((p * (channels // 2) + pair) * 8)
-    arrive(local_pulses * channels * 4)
+    load_halo = load(halo_hbm, halo_ref)
     load_halo_doppler = load(halo_doppler_hbm, halo_doppler_ref)
     load_mix = load(mix_hbm, mix_ref)
     load_tables = [
-        load(reach_hbm, reach_ref),
-        load(square_hbm, square_ref),
+        load(shift_hbm, shift_ref),
         load(cos_hbm, cos_ref),
         load(sin_hbm, sin_ref),
     ]
@@ -719,10 +741,10 @@
             spectra[c, half * LANES : (half + 1) * LANES, :] = dot_right(z.T, doppler_ref)
     groups = local_pulses * channels * MIG // LANES
     per_group = LANES // (MIG * channels)
-    arrivals[-1].wait()
+    load_halo.wait()
     load_halo_doppler.wait()
     h = jnp.concatenate(
-        [rows_of(local_pulses * channels * 4 + j) for j in range(2 * groups)], axis=0
+        [halo_ref[pl.ds(j, sources, stride=2 * groups), :] for j in range(2 * groups)], axis=0
     ).T
     step = channels * MIG
     halo = dot_right(h[:step], halo_doppler_ref.at[0])
@@ -734,16 +756,17 @@
     mix_channels(spectra, mix_ref, unfolded, bins + MIG, 0)
     for copy in load_tables:
         copy.wait()
-    migrate_rows(unfolded, cos_ref, sin_ref, reach_ref, square_ref, focused, bins)
+    migrate_rows(unfolded, cos_ref, sin_ref, shift_ref, focused, bins)
     for copy in load_final:
         copy.wait()
     stores = []
-    for k in range(bins // LANES):
-        at = slice(k * LANES, (k + 1) * LANES)
+    piece = LANES // 2
+    for k in range(bins // piece):
+        at = slice(k * piece, (k + 1) * piece)
         real, imag = inverse_rows(focused, final_ref, twiddle_ref, at)
         image_ref[0, at, :] = real
         image_ref[1, at, :] = imag
-        rows = pl.ds(k * LANES, LANES)
+        rows = pl.ds(k * piece, piece)
         copy = pltpu.make_async_copy(
             image_ref.at[:, rows], out_hbm.at[:, rows], store_sems.at[k]
         )
@@ -839,7 +862,7 @@
     x = raw_echoes.reshape(signals, 2, lead, LANES).transpose(0, 2, 1, 3)
     x = x.reshape(signals, 2 * lead, LANES)
     chirp = chirp_spectrum.reshape(2, lead, LANES).transpose(1, 0, 2).reshape(2 * lead, LANES)
-    block = signals * 4 + HALO_ROWS
+    block = signals * 4
     tables = (bins, doppler_bins)
     by_lane = (bins // LANES, LANES)
     operands = (
@@ -858,16 +881,16 @@
         delays.reshape(1, channels),
         order_f,
     )
-    received, cosine, sine, reach, square, mix = pl.pallas_call(
+    received, halo_received, cosine, sine, shift, mix = pl.pallas_call(
         functools.partial(
             compress_kernel, (local_pulses, channels, lead, devices, inner, doppler_bins)
         ),
         out_shape=(
             jax.ShapeDtypeStruct((devices, block, LANES), jnp.float32),
+            jax.ShapeDtypeStruct((devices, 2 * groups, LANES), jnp.float32),
             jax.ShapeDtypeStruct(tables, jnp.float32),
             jax.ShapeDtypeStruct(tables, jnp.float32),
             jax.ShapeDtypeStruct(tables, jnp.int32),
-            jax.ShapeDtypeStruct((bins, LANES), jnp.int32),
             jax.ShapeDtypeStruct((2, channels * channels, pulses), jnp.float32),
         ),
         in_specs=[hbm()] * len(operands),
@@ -875,17 +898,17 @@
         scratch_shapes=[pltpu.VMEM(value.shape, value.dtype) for value in operands]
         + [
             pltpu.VMEM((devices, block, LANES), jnp.float32),
+            pltpu.VMEM((devices, 2 * groups, LANES), jnp.float32),
             pltpu.VMEM((3, bins, LANES), jnp.float32),
             pltpu.VMEM(tables, jnp.float32),
             pltpu.VMEM(tables, jnp.float32),
             pltpu.VMEM(tables, jnp.int32),
-            pltpu.VMEM((bins, LANES), jnp.int32),
             pltpu.VMEM((2, channels * channels, pulses), jnp.float32),
             pltpu.SemaphoreType.DMA((len(operands) + local_pulses - 1,)),
-            pltpu.SemaphoreType.DMA((5,)),
-            pltpu.SemaphoreType.DMA,
-            pltpu.SemaphoreType.DMA((2, devices)),
-            pltpu.SemaphoreType.DMA((2, devices)),
+            pltpu.SemaphoreType.DMA((4,)),
+            pltpu.SemaphoreType.DMA((2,)),
+            pltpu.SemaphoreType.DMA((3, devices)),
+            pltpu.SemaphoreType.DMA((3, devices)),
         ],
         compiler_params=pltpu.CompilerParams(
             collective_id=0, has_side_effects=True, vmem_limit_bytes=KERNEL_VMEM
@@ -894,11 +917,11 @@
     )(*operands)
     inputs = (
         received,
+        halo_received.reshape(devices * 2 * groups, LANES),
         split_constant(to_doppler),
         halo_doppler,
         mix,
-        reach,
-        square,
+        shift,
         cosine,
         sine,
         final,
@@ -916,8 +939,8 @@
             pltpu.VMEM((bins, 2 * doppler_bins), jnp.float32),
             pltpu.VMEM((2, bins, doppler_bins), jnp.float32),
             pltpu.SemaphoreType.DMA((len(inputs) - 1,)),
-            pltpu.SemaphoreType.DMA((channels // 2 * local_pulses + 1,)),
-            pltpu.SemaphoreType.DMA((bins // LANES,)),
+            pltpu.SemaphoreType.DMA((channels // 2 * local_pulses,)),
+            pltpu.SemaphoreType.DMA((2 * bins // LANES,)),
         ],
         compiler_params=pltpu.CompilerParams(vmem_limit_bytes=KERNEL_VMEM),
         name="azimuth_focus",

time: 41.3 us -> 42.2 us (1.022)
  Pallas kernels: 41.1 us -> 42 us
    pallas_call x1, Pallas kernels: 33.8 us -> 34.9 us  [blocked_local(): pl.pallas_call(functools.partial(compress_kernel, (local_pulses, channels...]
where the time goes in v7:
time: 42.2 us; the launch traced here: 42 us
  Pallas kernels  42 us (100%)
    pallas_call x1, Pallas kernels, blocked_local(): pl.pallas_call(functools.partial(compress_kernel, (local_pulses, channels...  34.9 us
    pallas_call x1, Pallas kernels, blocked_local(): pl.pallas_call(functools.partial(azimuth_kernel, (devices, local_pulses,...  7.05 us

profile of v7, /device:TPU:0, one launch (start us, length us, event | category | flops | bytes accessed | tf_op | source)
XLA Modules:
  0.0 42.0 jit_solution(10497985844997036486)
XLA Ops:
  0.0 34.9 %compress_exchange.1 = (f32[32,64,128]{2,1,0:T(8,128)}, f32[32,4,128]{2,1,0:T(4,128)}, f32[256,512]{1,0:T(8,128)}, f32[256,512]{1,0:T(8,128)}, s32[256,512]{1,0:T(8,128)}, /*index=5*/f32[2,16,128]{2,1,0:T(8,128)}) custom-call(f32[16,128,128]{2,1,0:T(8,128)} %bitcast.16, f32[128,128]{1,0:T(8,128)} %bitcast.18, f32[2,128]{1,0:T(2,128)} %bitcast.20, ...), custom_call_target="tpu_custom_call" | custom-call | tf_op jit(solution)/shard_map/compress_exchange/pallas_call | solution.py:884
  35.0 7.0 %azimuth_focus.1 = f32[2,256,512]{2,1,0:T(8,128)} custom-call(f32[32,64,128]{2,1,0:T(8,128)} %get-tuple-element.11.recv_hbm, f32[128,128]{1,0:T(8,128)} %bitcast.17, bf16[2,256,256]{2,1,0:T(8,128)(2,1)} %constant.29.clone.doppler_hbm, bf16[2,2,128,256]{3,2,1,0:T(8,128)(2,1)} %constant.30.clone.halo_doppler_hbm, f32[2,16,128]{2,1,0:T(8,128)} %get-tuple-element.13.mix_hbm, ...), custom_call_target="tpu_custom_call" | custom-call | tf_op jit(solution)/shard_map/azimuth_focus/pallas_call | solution.py:930

commit v8 on v7

--- a/solution.py
+++ b/solution.py
@@ -212,7 +212,9 @@
 
 def dot_right(values, matrix):
     high, low = split(values)
-    return dot(high, matrix[0]) + (dot(low, matrix[0]) + dot(high, matrix[1]))
+    rows = values.shape[0]
+    both = dot(jnp.concatenate([high, low], axis=0), matrix[0])
+    return both[:rows] + (both[rows:] + dot(high, matrix[1]))
 
 
 def dot_left(matrix, values):
@@ -389,7 +391,6 @@
     delays_hbm,
     order_hbm,
     recv_ref,
-    halo_recv_ref,
     cos_hbm,
     sin_hbm,
     shift_hbm,
@@ -409,7 +410,6 @@
     delays_ref,
     order_ref,
     send_ref,
-    send_halo_ref,
     rows_ref,
     cos_ref,
     sin_ref,
@@ -417,7 +417,7 @@
     mix_ref,
     load_sems,
     store_sems,
-    local_sems,
+    local_sem,
     send_sems,
     recv_sems,
 ):
@@ -466,23 +466,17 @@
     load_order = start_load(order_hbm, order_ref)
     lax.fori_loop(1, devices, greet, 0)
 
-    rows = pulses * channels * 4
+    rows = pulses * channels * 4 + HALO_ROWS
     cut = channels * 4
-
-    def parts(chunk, target):
-        if chunk == 2:
-            return send_halo_ref.at[target], halo_recv_ref.at[mine]
-        at = pl.ds(0, cut) if chunk == 0 else pl.ds(cut, rows - cut)
-        return send_ref.at[target, at], recv_ref.at[mine, at]
 
     def remote(chunk, i):
         far = lax.div(i + 1, 2)
         step = devices // 2 + far - 2 * far * lax.rem(i, 2)
         target = lax.rem(mine + step, devices)
-        source, landing = parts(chunk, target)
+        at = pl.ds(0, cut) if chunk == 0 else pl.ds(cut, rows - cut)
         return pltpu.make_async_remote_copy(
-            src_ref=source,
-            dst_ref=landing,
+            src_ref=send_ref.at[target, at],
+            dst_ref=recv_ref.at[mine, at],
             send_sem=send_sems.at[chunk, step],
             recv_sem=recv_sems.at[chunk, step],
             device_id=place(target),
@@ -562,21 +556,16 @@
         if p == 0:
             pl.semaphore_wait(barrier, devices - 1)
             send(0)
-    send(1)
     load_halo.wait()
     w = dot_left(halo_ref, jnp.concatenate(packs, axis=1))
     row = lax.broadcasted_iota(jnp.int32, (devices * HALO_ROWS, LANES), 0) % HALO_ROWS
     total = w[:, :LANES]
     for g in range(1, groups):
         total = jnp.where(row // 2 == g, w[:, g * LANES : (g + 1) * LANES], total)
-    send_halo_ref[...] = total.reshape(devices, HALO_ROWS, LANES)[:, : 2 * groups, :]
-    send(2)
-    own = [
-        pltpu.make_async_copy(send_ref.at[mine], recv_ref.at[mine], local_sems.at[0]),
-        pltpu.make_async_copy(send_halo_ref.at[mine], halo_recv_ref.at[mine], local_sems.at[1]),
-    ]
-    for copy in own:
-        copy.start()
+    send_ref[:, pulses * channels * 4 :, :] = total.reshape(devices, HALO_ROWS, LANES)
+    send(1)
+    own = pltpu.make_async_copy(send_ref.at[mine], recv_ref.at[mine], local_sem)
+    own.start()
 
     load_reconstruction.wait()
     load_delays.wait()
@@ -641,11 +630,10 @@
         stores.append(copy)
     for copy in stores:
         copy.wait()
-    for copy in own:
-        copy.wait()
+    own.wait()
 
     def finish(i, carry):
-        for chunk in range(3):
+        for chunk in range(2):
             copy = remote(chunk, i)
             copy.wait_send()
             copy.wait_recv()
@@ -657,7 +645,6 @@
 def azimuth_kernel(
     sizes,
     recv_hbm,
-    halo_hbm,
     doppler_hbm,
     halo_doppler_hbm,
     mix_hbm,
@@ -668,7 +655,6 @@
     twiddle_hbm,
     out_hbm,
     recv_ref,
-    halo_ref,
     doppler_ref,
     halo_doppler_ref,
     mix_ref,
@@ -686,7 +672,7 @@
     store_sems,
 ):
     sources, local_pulses, channels, bins = sizes
-    block = local_pulses * channels * 4
+    block = local_pulses * channels * 4 + HALO_ROWS
     arrivals = []
 
     def arrive(row):
@@ -709,7 +695,7 @@
     for pair in range(channels // 2):
         for p in range(local_pulses):
             arrive((p * (channels // 2) + pair) * 8)
-    load_halo = load(halo_hbm, halo_ref)
+    arrive(local_pulses * channels * 4)
     load_halo_doppler = load(halo_doppler_hbm, halo_doppler_ref)
     load_mix = load(mix_hbm, mix_ref)
     load_tables = [
@@ -724,27 +710,32 @@
     def rows_of(start):
         return flat[pl.ds(start, sources, stride=block), :]
 
-    load_doppler.wait()
-    for c in range(channels):
-        if c % 2 == 0:
-            for p in range(local_pulses):
-                arrivals[c // 2 * local_pulses + p].wait()
-        for half in range(bins // LANES):
-            z = jnp.concatenate(
-                [
-                    rows_of(p * channels * 4 + c * 4 + part * 2 + half)
-                    for part in range(2)
-                    for p in range(local_pulses)
-                ],
-                axis=0,
-            )
-            spectra[c, half * LANES : (half + 1) * LANES, :] = dot_right(z.T, doppler_ref)
+    for pair in range(channels // 2):
+        for p in range(local_pulses):
+            arrivals[pair * local_pulses + p].wait()
+        turned = []
+        for c in (2 * pair, 2 * pair + 1):
+            for half in range(bins // LANES):
+                z = jnp.concatenate(
+                    [
+                        rows_of(p * channels * 4 + c * 4 + part * 2 + half)
+                        for part in range(2)
+                        for p in range(local_pulses)
+                    ],
+                    axis=0,
+                )
+                turned.append(z.T)
+        if pair == 0:
+            load_doppler.wait()
+        result = dot_right(jnp.concatenate(turned, axis=0), doppler_ref)
+        spectra[2 * pair, :bins, :] = result[:bins]
+        spectra[2 * pair + 1, :bins, :] = result[bins:]
     groups = local_pulses * channels * MIG // LANES
     per_group = LANES // (MIG * channels)
-    load_halo.wait()
+    arrivals[-1].wait()
     load_halo_doppler.wait()
     h = jnp.concatenate(
-        [halo_ref[pl.ds(j, sources, stride=2 * groups), :] for j in range(2 * groups)], axis=0
+        [rows_of(local_pulses * channels * 4 + j) for j in range(2 * groups)], axis=0
     ).T
     step = channels * MIG
     halo = dot_right(h[:step], halo_doppler_ref.at[0])
@@ -760,13 +751,12 @@
     for copy in load_final:
         copy.wait()
     stores = []
-    piece = LANES // 2
-    for k in range(bins // piece):
-        at = slice(k * piece, (k + 1) * piece)
+    for k in range(bins // LANES):
+        at = slice(k * LANES, (k + 1) * LANES)
         real, imag = inverse_rows(focused, final_ref, twiddle_ref, at)
         image_ref[0, at, :] = real
         image_ref[1, at, :] = imag
-        rows = pl.ds(k * piece, piece)
+        rows = pl.ds(k * LANES, LANES)
         copy = pltpu.make_async_copy(
             image_ref.at[:, rows], out_hbm.at[:, rows], store_sems.at[k]
         )
@@ -862,7 +852,7 @@
     x = raw_echoes.reshape(signals, 2, lead, LANES).transpose(0, 2, 1, 3)
     x = x.reshape(signals, 2 * lead, LANES)
     chirp = chirp_spectrum.reshape(2, lead, LANES).transpose(1, 0, 2).reshape(2 * lead, LANES)
-    block = signals * 4
+    block = signals * 4 + HALO_ROWS
     tables = (bins, doppler_bins)
     by_lane = (bins // LANES, LANES)
     operands = (
@@ -881,24 +871,22 @@
         delays.reshape(1, channels),
         order_f,
     )
-    received, halo_received, cosine, sine, shift, mix = pl.pallas_call(
+    received, cosine, sine, shift, mix = pl.pallas_call(
         functools.partial(
             compress_kernel, (local_pulses, channels, lead, devices, inner, doppler_bins)
         ),
         out_shape=(
             jax.ShapeDtypeStruct((devices, block, LANES), jnp.float32),
-            jax.ShapeDtypeStruct((devices, 2 * groups, LANES), jnp.float32),
             jax.ShapeDtypeStruct(tables, jnp.float32),
             jax.ShapeDtypeStruct(tables, jnp.float32),
             jax.ShapeDtypeStruct(tables, jnp.int32),
             jax.ShapeDtypeStruct((2, channels * channels, pulses), jnp.float32),
         ),
         in_specs=[hbm()] * len(operands),
-        out_specs=(hbm(),) * 6,
+        out_specs=(hbm(),) * 5,
         scratch_shapes=[pltpu.VMEM(value.shape, value.dtype) for value in operands]
         + [
             pltpu.VMEM((devices, block, LANES), jnp.float32),
-            pltpu.VMEM((devices, 2 * groups, LANES), jnp.float32),
             pltpu.VMEM((3, bins, LANES), jnp.float32),
             pltpu.VMEM(tables, jnp.float32),
             pltpu.VMEM(tables, jnp.float32),
@@ -906,9 +894,9 @@
             pltpu.VMEM((2, channels * channels, pulses), jnp.float32),
             pltpu.SemaphoreType.DMA((len(operands) + local_pulses - 1,)),
             pltpu.SemaphoreType.DMA((4,)),
-            pltpu.SemaphoreType.DMA((2,)),
-            pltpu.SemaphoreType.DMA((3, devices)),
-            pltpu.SemaphoreType.DMA((3, devices)),
+            pltpu.SemaphoreType.DMA,
+            pltpu.SemaphoreType.DMA((2, devices)),
+            pltpu.SemaphoreType.DMA((2, devices)),
         ],
         compiler_params=pltpu.CompilerParams(
             collective_id=0, has_side_effects=True, vmem_limit_bytes=KERNEL_VMEM
@@ -917,7 +905,6 @@
     )(*operands)
     inputs = (
         received,
-        halo_received.reshape(devices * 2 * groups, LANES),
         split_constant(to_doppler),
         halo_doppler,
         mix,
@@ -939,8 +926,8 @@
             pltpu.VMEM((bins, 2 * doppler_bins), jnp.float32),
             pltpu.VMEM((2, bins, doppler_bins), jnp.float32),
             pltpu.SemaphoreType.DMA((len(inputs) - 1,)),
-            pltpu.SemaphoreType.DMA((channels // 2 * local_pulses,)),
-            pltpu.SemaphoreType.DMA((2 * bins // LANES,)),
+            pltpu.SemaphoreType.DMA((channels // 2 * local_pulses + 1,)),
+            pltpu.SemaphoreType.DMA((bins // LANES,)),
         ],
         compiler_params=pltpu.CompilerParams(vmem_limit_bytes=KERNEL_VMEM),
         name="azimuth_focus",

time: 42.2 us -> 41.2 us (0.976)
  Pallas kernels: 42 us -> 41.1 us
    pallas_call x1, Pallas kernels: 34.9 us -> 33.8 us  [blocked_local(): pl.pallas_call(functools.partial(compress_kernel, (local_pulses, channels...]
where the time goes in v8:
time: 41.2 us; the launch traced here: 41.1 us
  Pallas kernels  41.1 us (100%)
    pallas_call x1, Pallas kernels, blocked_local(): pl.pallas_call(functools.partial(compress_kernel, (local_pulses, channels...  33.8 us
    pallas_call x1, Pallas kernels, blocked_local(): pl.pallas_call(functools.partial(azimuth_kernel, (devices, local_pulses,...  7.26 us

profile of v8, /device:TPU:0, one launch (start us, length us, event | category | flops | bytes accessed | tf_op | source)
XLA Modules:
  0.0 41.1 jit_solution(14440416599004157201)
XLA Ops:
  0.0 33.8 %compress_exchange.1 = (f32[32,72,128]{2,1,0:T(8,128)}, f32[256,512]{1,0:T(8,128)}, f32[256,512]{1,0:T(8,128)}, s32[256,512]{1,0:T(8,128)}, f32[2,16,128]{2,1,0:T(8,128)}) custom-call(f32[16,128,128]{2,1,0:T(8,128)} %bitcast.15, f32[128,128]{1,0:T(8,128)} %bitcast.16, f32[2,128]{1,0:T(2,128)} %bitcast.18, s32[2,128]{1,0:T(2,128)} %bitcast.19, ...), custom_call_target="tpu_custom_call" | custom-call | tf_op jit(solution)/shard_map/compress_exchange/pallas_call | solution.py:874
  33.8 7.3 %azimuth_focus.1 = f32[2,256,512]{2,1,0:T(8,128)} custom-call(f32[32,72,128]{2,1,0:T(8,128)} %get-tuple-element.10.recv_hbm, bf16[2,256,256]{2,1,0:T(8,128)(2,1)} %constant.29.clone.doppler_hbm, bf16[2,2,128,256]{3,2,1,0:T(8,128)(2,1)} %constant.30.clone.halo_doppler_hbm, f32[2,16,128]{2,1,0:T(8,128)} %get-tuple-element.11.mix_hbm, ...), custom_call_target="tpu_custom_call" | custom-call | tf_op jit(solution)/shard_map/azimuth_focus/pallas_call | solution.py:917

commit v9 on v8

--- a/solution.py
+++ b/solution.py
@@ -212,9 +212,7 @@
 
 def dot_right(values, matrix):
     high, low = split(values)
-    rows = values.shape[0]
-    both = dot(jnp.concatenate([high, low], axis=0), matrix[0])
-    return both[:rows] + (both[rows:] + dot(high, matrix[1]))
+    return dot(high, matrix[0]) + (dot(low, matrix[0]) + dot(high, matrix[1]))
 
 
 def dot_left(matrix, values):
@@ -668,21 +666,10 @@
     focused,
     image_ref,
     load_sems,
-    recv_sems,
     store_sems,
 ):
     sources, local_pulses, channels, bins = sizes
     block = local_pulses * channels * 4 + HALO_ROWS
-    arrivals = []
-
-    def arrive(row):
-        at = pl.ds(row, 8)
-        copy = pltpu.make_async_copy(
-            recv_hbm.at[:, at], recv_ref.at[:, at], recv_sems.at[len(arrivals)]
-        )
-        copy.start()
-        arrivals.append(copy)
-
     loads = []
 
     def load(source, target):
@@ -692,10 +679,7 @@
         return copy
 
     load_doppler = load(doppler_hbm, doppler_ref)
-    for pair in range(channels // 2):
-        for p in range(local_pulses):
-            arrive((p * (channels // 2) + pair) * 8)
-    arrive(local_pulses * channels * 4)
+    load_recv = load(recv_hbm, recv_ref)
     load_halo_doppler = load(halo_doppler_hbm, halo_doppler_ref)
     load_mix = load(mix_hbm, mix_ref)
     load_tables = [
@@ -710,29 +694,21 @@
     def rows_of(start):
         return flat[pl.ds(start, sources, stride=block), :]
 
-    for pair in range(channels // 2):
-        for p in range(local_pulses):
-            arrivals[pair * local_pulses + p].wait()
-        turned = []
-        for c in (2 * pair, 2 * pair + 1):
-            for half in range(bins // LANES):
-                z = jnp.concatenate(
-                    [
-                        rows_of(p * channels * 4 + c * 4 + part * 2 + half)
-                        for part in range(2)
-                        for p in range(local_pulses)
-                    ],
-                    axis=0,
-                )
-                turned.append(z.T)
-        if pair == 0:
-            load_doppler.wait()
-        result = dot_right(jnp.concatenate(turned, axis=0), doppler_ref)
-        spectra[2 * pair, :bins, :] = result[:bins]
-        spectra[2 * pair + 1, :bins, :] = result[bins:]
+    load_doppler.wait()
+    load_recv.wait()
+    for c in range(channels):
+        for half in range(bins // LANES):
+            z = jnp.concatenate(
+                [
+                    rows_of(p * channels * 4 + c * 4 + part * 2 + half)
+                    for part in range(2)
+                    for p in range(local_pulses)
+                ],
+                axis=0,
+            )
+            spectra[c, half * LANES : (half + 1) * LANES, :] = dot_right(z.T, doppler_ref)
     groups = local_pulses * channels * MIG // LANES
     per_group = LANES // (MIG * channels)
-    arrivals[-1].wait()
     load_halo_doppler.wait()
     h = jnp.concatenate(
         [rows_of(local_pulses * channels * 4 + j) for j in range(2 * groups)], axis=0
@@ -751,12 +727,13 @@
     for copy in load_final:
         copy.wait()
     stores = []
-    for k in range(bins // LANES):
-        at = slice(k * LANES, (k + 1) * LANES)
+    piece = LANES // 2
+    for k in range(bins // piece):
+        at = slice(k * piece, (k + 1) * piece)
         real, imag = inverse_rows(focused, final_ref, twiddle_ref, at)
         image_ref[0, at, :] = real
         image_ref[1, at, :] = imag
-        rows = pl.ds(k * LANES, LANES)
+        rows = pl.ds(k * piece, piece)
         copy = pltpu.make_async_copy(
             image_ref.at[:, rows], out_hbm.at[:, rows], store_sems.at[k]
         )
@@ -925,9 +902,8 @@
             pltpu.VMEM((bins + MIG, 2 * doppler_bins), jnp.float32),
             pltpu.VMEM((bins, 2 * doppler_bins), jnp.float32),
             pltpu.VMEM((2, bins, doppler_bins), jnp.float32),
-            pltpu.SemaphoreType.DMA((len(inputs) - 1,)),
-            pltpu.SemaphoreType.DMA((channels // 2 * local_pulses + 1,)),
-            pltpu.SemaphoreType.DMA((bins // LANES,)),
+            pltpu.SemaphoreType.DMA((len(inputs),)),
+            pltpu.SemaphoreType.DMA((2 * bins // LANES,)),
         ],
         compiler_params=pltpu.CompilerParams(vmem_limit_bytes=KERNEL_VMEM),
         name="azimuth_focus",

time: 41.2 us -> 40.4 us (0.981)
  Pallas kernels: 41.1 us -> 40.2 us
    pallas_call x1, Pallas kernels: 7.26 us -> 6.37 us  [blocked_local(): pl.pallas_call(functools.partial(azimuth_kernel, (devices, local_pulses,...]
where the time goes in v9:
time: 40.4 us; the launch traced here: 40.2 us
  Pallas kernels  40.2 us (100%)
    pallas_call x1, Pallas kernels, blocked_local(): pl.pallas_call(functools.partial(compress_kernel, (local_pulses, channels...  33.8 us
    pallas_call x1, Pallas kernels, blocked_local(): pl.pallas_call(functools.partial(azimuth_kernel, (devices, local_pulses,...  6.37 us

profile of v9, /device:TPU:0, one launch (start us, length us, event | category | flops | bytes accessed | tf_op | source)
XLA Modules:
  0.0 40.2 jit_solution(317597479024666793)
XLA Ops:
  0.0 33.8 %compress_exchange.1 = (f32[32,72,128]{2,1,0:T(8,128)}, f32[256,512]{1,0:T(8,128)}, f32[256,512]{1,0:T(8,128)}, s32[256,512]{1,0:T(8,128)}, f32[2,16,128]{2,1,0:T(8,128)}) custom-call(f32[16,128,128]{2,1,0:T(8,128)} %bitcast.15, f32[128,128]{1,0:T(8,128)} %bitcast.16, f32[2,128]{1,0:T(2,128)} %bitcast.18, s32[2,128]{1,0:T(2,128)} %bitcast.19, ...), custom_call_target="tpu_custom_call" | custom-call | tf_op jit(solution)/shard_map/compress_exchange/pallas_call | solution.py:851
  33.8 6.4 %azimuth_focus.1 = f32[2,256,512]{2,1,0:T(8,128)} custom-call(f32[32,72,128]{2,1,0:T(8,128)} %get-tuple-element.10.recv_hbm, bf16[2,256,256]{2,1,0:T(8,128)(2,1)} %constant.29.clone.doppler_hbm, bf16[2,2,128,256]{3,2,1,0:T(8,128)(2,1)} %constant.30.clone.halo_doppler_hbm, f32[2,16,128]{2,1,0:T(8,128)} %get-tuple-element.11.mix_hbm, ...), custom_call_target="tpu_custom_call" | custom-call | tf_op jit(solution)/shard_map/azimuth_focus/pallas_call | solution.py:894
